TPU v7x, 128 devices: a whole 4x4x4 slice. The times are simulated.
128 devices in a mesh: wide: 32 (over y, x, core), narrow: 4 (over z).
Axes of the slice: x: 4, y: 4, z: 4, core: 2. Of those that a mesh axis runs over, the one named last changes fastest.
Arguments:
- cache: bfloat16 [16, 16384, 8, 128], P(None, 'wide', 'narrow'), may hold values from -24 to 24
- lengths: int32 [16], replicated, may hold values from 2 to 16384, as said below
- queries: bfloat16 [3, 2048, 4096], P(None, 'wide', 'narrow'), may hold values from -30 to 30
- new_kv: bfloat16 [3, 2048, 8, 128], P(None, 'wide', 'narrow'), may hold values from -6 to 6
- sinks: float32 [64], replicated, may hold values from 8 to 14
- residual: bfloat16 [3, 2048, 2880], P(None, ('wide', 'narrow')), may hold values from -6 to 6
- norm_gain: bfloat16 [2880], replicated, may hold values from 0.5 to 1.5
- w_out: bfloat16 [4096, 2880], P('narrow'), may hold values from -0.09375 to 0.09375
- w_router: bfloat16 [2880, 64], replicated, may hold values from -0.109375 to 0.109375
- expert_ids: int32 [3, 2048, 4], P(None, ('wide', 'narrow')), may hold values from 0 to 63, all different within a row; in each aligned block of 16 rows (0 to 15, 16 to 31, ..., all dimensions but the last counted through in order) at most 2 rows name the same one
- w_gate_up: bfloat16 [128, 2880, 2, 720], P(('wide', 'narrow')), may hold values from -0.3125 to 0.3125
- w_down: bfloat16 [128, 720, 2880], P(('wide', 'narrow')), may hold values from -0.0546875 to 0.0546875
Outputs:
- layer_out: bfloat16 [3, 2048, 2880], P(None, ('wide', 'narrow'))
Inputs may be any that keep to these rules, and one draw needn't show every extreme that they name: `lengths`: the longest request uses all 16384 positions. `expert_ids`: each row names 4 different experts; within each aligned block of 16 rows of a step no expert is named more than 2 times, a bound that some block reaches.
All inputs are finite; a program needn't handle non-finite values.
Results may differ from a plain program's by a relative error of at most 0.024.
Values may be sent and summed in bfloat16 or wider, within the bound.
No kernel may reach another device: no remote copies, remote signals or barrier semaphores. Data moves between devices by JAX's collectives and lax.ppermute only.
A program may use at most 128 MiB of HBM per device.

v0:
```python
import math

import jax
import jax.numpy as jnp
from jax import lax
from jax.sharding import PartitionSpec as P


def partner(block, axis, distance):
    count = lax.axis_size(axis)
    route = []
    for low in range(count):
        high = low | 1 << distance
        if high != low and high < count:
            route += [(low, high), (high, low)]
    return lax.ppermute(block, axis, route)


def absorb(running, both_q, key_rows, value_rows, allowed, score_scale):
    old_peak, old_total, old_acc = running
    scores = (
        jnp.einsum("rhge,khe->rhgk", both_q, key_rows, preferred_element_type=jnp.float32)
        * score_scale
    )
    allow_mask = allowed[:, None, None, :]
    masked = jnp.where(allow_mask, scores, -1e30)
    new_peak = jnp.maximum(old_peak, jnp.max(masked, axis=-1))
    weights = jnp.where(allow_mask, jnp.exp(masked - new_peak[..., None]), 0.0)
    rescale = jnp.exp(old_peak - new_peak)
    new_total = old_total * rescale + jnp.sum(weights, axis=-1)
    new_acc = old_acc * rescale[..., None] + jnp.einsum(
        "rhgk,khe->rhge",
        weights.astype(jnp.bfloat16),
        value_rows,
        preferred_element_type=jnp.float32,
    )
    return (new_peak, new_total, new_acc)


def send_rows(outgoing):
    return lax.all_to_all(outgoing, ("wide", "narrow"), split_axis=0, concat_axis=0, tiled=True)


def send_back(results):
    return lax.all_to_all(
        results.astype(jnp.bfloat16), ("wide", "narrow"), split_axis=0, concat_axis=0, tiled=True
    ).astype(results.dtype)


def shards(
    cache,
    lengths,
    queries,
    new_kv,
    sinks,
    residual,
    norm_gain,
    w_out,
    w_router,
    expert_ids,
    w_gate_up,
    w_down,
):
    wide_count = lax.axis_size("wide")
    narrow_count = lax.axis_size("narrow")
    devices = wide_count * narrow_count
    wide_index = lax.axis_index("wide")
    narrow_index = lax.axis_index("narrow")
    pair_side = wide_index % 2
    request = wide_index // 2
    requests = cache.shape[0]
    block_len = cache.shape[1]
    kv_local = cache.shape[2]
    packed_width = cache.shape[3]
    head_dim = packed_width // 2
    half_block = block_len // 2
    pieces = cache.reshape(requests * 2, half_block, kv_local, packed_width)
    regrouped = lax.all_to_all(pieces, "wide", split_axis=0, concat_axis=0, tiled=True)
    key_count = wide_count * half_block
    key_pos = (
        jnp.arange(wide_count, dtype=jnp.int32)[:, None] * block_len
        + pair_side * half_block
        + jnp.arange(half_block, dtype=jnp.int32)[None, :]
    ).reshape(key_count)
    key_span = 2048
    key_blocks = regrouped.reshape(key_count // key_span, key_span, kv_local, packed_width)
    pos_blocks = key_pos.reshape(key_count // key_span, key_span)
    cache_length = lengths[request]
    steps = queries.shape[0]
    own_rows = queries.shape[1]
    q_width = queries.shape[2]
    groups = q_width // (kv_local * head_dim)
    local_heads = kv_local * groups
    local_sink = lax.dynamic_slice_in_dim(
        sinks, narrow_index * local_heads, local_heads, 0
    ).reshape(kv_local, groups)
    rows_req = 2 * own_rows
    rows_dev = own_rows // narrow_count
    score_scale = 1.0 / math.sqrt(head_dim)
    model_dim = residual.shape[2]
    experts = w_router.shape[1]
    top_k = expert_ids.shape[2]
    capacity = rows_dev * top_k * 2 // experts
    eff_half = w_down.shape[1]
    assigned = rows_dev * top_k
    earlier = (jnp.arange(assigned)[:, None] > jnp.arange(assigned)[None, :]).astype(jnp.float32)
    slot_range = jnp.arange(experts * capacity, dtype=jnp.int32)
    expert_range = jnp.arange(experts, dtype=jnp.int32)
    gain_wide = norm_gain.astype(jnp.float32)
    gate_up_local = w_gate_up[0].reshape(model_dim, 2 * eff_half)
    down_local = w_down[0]
    start_peak = jnp.broadcast_to(
        jnp.where(pair_side == 0, local_sink, -1e30)[None], (rows_req, kv_local, groups)
    )
    start_total = jnp.broadcast_to(
        jnp.where(pair_side == 0, 1.0, 0.0).astype(jnp.float32), (rows_req, kv_local, groups)
    )
    outputs = []
    for step_index in range(steps):
        own_q = queries[step_index]
        other_q = partner(own_q, "wide", 0)
        lower_q = jnp.where(pair_side == 0, own_q, other_q)
        upper_q = jnp.where(pair_side == 0, other_q, own_q)
        both_q = jnp.concatenate([lower_q, upper_q], axis=0).reshape(
            rows_req, kv_local, groups, head_dim
        )
        query_pos = cache_length + rows_req * step_index + jnp.arange(rows_req, dtype=jnp.int32)
        initial = (
            start_peak,
            start_total,
            jnp.zeros((rows_req, kv_local, groups, head_dim), jnp.float32),
        )

        def cache_block(running, key_block):
            key_values, positions = key_block
            allowed = (positions < cache_length)[None, :]
            return (
                absorb(
                    running,
                    both_q,
                    key_values[:, :, :head_dim],
                    key_values[:, :, head_dim:],
                    allowed,
                    score_scale,
                ),
                0,
            )

        running, unused = lax.scan(cache_block, initial, (key_blocks, pos_blocks))
        recent = new_kv[: step_index + 1].reshape(
            (step_index + 1) * own_rows, kv_local, packed_width
        )
        recent_pos = (
            cache_length
            + rows_req * jnp.arange(step_index + 1, dtype=jnp.int32)[:, None]
            + pair_side * own_rows
            + jnp.arange(own_rows, dtype=jnp.int32)[None, :]
        ).reshape(-1)
        allowed = recent_pos[None, :] <= query_pos[:, None]
        run_peak, run_total, run_acc = absorb(
            running, both_q, recent[:, :, :head_dim], recent[:, :, head_dim:], allowed, score_scale
        )

        def keep_give(value):
            lower_rows = value[:own_rows]
            upper_rows = value[own_rows:]
            return (
                jnp.where(pair_side == 0, lower_rows, upper_rows),
                jnp.where(pair_side == 0, upper_rows, lower_rows),
            )

        keep_peak, give_peak = keep_give(run_peak)
        keep_total, give_total = keep_give(run_total)
        keep_acc, give_acc = keep_give(run_acc)
        got_peak, got_total, got_acc = (
            partner(give_peak.astype(jnp.bfloat16), "wide", 0).astype(give_peak.dtype),
            partner(give_total.astype(jnp.bfloat16), "wide", 0).astype(give_total.dtype),
            partner(give_acc.astype(jnp.bfloat16), "wide", 0).astype(give_acc.dtype),
        )
        joint_peak = jnp.maximum(keep_peak, got_peak)
        mine_scale = jnp.exp(keep_peak - joint_peak)
        their_scale = jnp.exp(got_peak - joint_peak)
        denominator = keep_total * mine_scale + got_total * their_scale
        numerator = keep_acc * mine_scale[..., None] + got_acc * their_scale[..., None]
        attended = (
            (numerator / denominator[..., None]).reshape(own_rows, q_width).astype(jnp.bfloat16)
        )
        projected = lax.psum_scatter(
            jnp.dot(attended, w_out, preferred_element_type=jnp.float32).astype(jnp.bfloat16),
            "narrow",
            scatter_dimension=0,
            tiled=True,
        ).astype(jnp.float32)
        hidden = residual[step_index].astype(jnp.float32) + projected
        normed = (
            hidden
            * lax.rsqrt(jnp.mean(hidden * hidden, axis=-1, keepdims=True) + 1e-05)
            * gain_wide
        ).astype(jnp.bfloat16)
        logits = jnp.dot(normed, w_router, preferred_element_type=jnp.float32)
        chosen_ids = expert_ids[step_index]
        picked = (chosen_ids[:, :, None] == expert_range[None, None, :]).astype(jnp.float32)
        chosen = jnp.sum(picked * logits[:, None, :], axis=-1)
        gate_weights = jnp.exp(chosen)
        gate_weights = gate_weights / jnp.sum(gate_weights, axis=-1, keepdims=True)
        flat_picks = picked.reshape(assigned, experts)
        before = jnp.dot(earlier, flat_picks, precision=lax.Precision.HIGHEST)
        slot_rank = jnp.sum(flat_picks * before, axis=-1).astype(jnp.int32)
        slot_index = chosen_ids.reshape(assigned) * capacity + slot_rank
        placement = (
            (slot_index[:, None] == slot_range[None, :])
            .astype(jnp.float32)
            .reshape(rows_dev, top_k, experts * capacity)
        )
        chooser = jnp.sum(placement, axis=1).astype(jnp.bfloat16)
        blender = jnp.sum(placement * gate_weights[:, :, None], axis=1)
        packed = jnp.einsum(
            "rs,rd->sd", chooser, normed, preferred_element_type=jnp.float32
        ).astype(jnp.bfloat16)
        outgoing = jnp.broadcast_to(
            packed.reshape(experts, 1, capacity, model_dim), (experts, 2, capacity, model_dim)
        ).reshape(devices, capacity, model_dim)
        arrived = send_rows(outgoing)
        rows_in = arrived.reshape(devices * capacity, model_dim)
        gate_up = jnp.dot(rows_in, gate_up_local, preferred_element_type=jnp.float32)
        gate_part = jnp.minimum(gate_up[:, :eff_half], 7.0)
        up_part = jnp.clip(gate_up[:, eff_half:], -7.0, 7.0)
        activation = (gate_part * jax.nn.sigmoid(1.702 * gate_part) * (up_part + 1.0)).astype(
            jnp.bfloat16
        )
        partial_value = jnp.dot(activation, down_local, preferred_element_type=jnp.float32).reshape(
            devices, capacity, model_dim
        )
        returned = send_back(partial_value)
        expert_out = jnp.sum(returned.reshape(experts, 2, capacity, model_dim), axis=1).reshape(
            experts * capacity, model_dim
        )
        combined = jnp.dot(
            blender, expert_out, precision=lax.Precision.HIGHEST, preferred_element_type=jnp.float32
        )
        outputs.append((hidden + combined).astype(jnp.bfloat16))
    return jnp.stack(outputs)


def solution(mesh):
    return jax.shard_map(
        shards,
        mesh=mesh,
        in_specs=(
            P(None, "wide", "narrow", None),
            P(),
            P(None, "wide", "narrow"),
            P(None, "wide", "narrow", None),
            P(),
            P(None, ("wide", "narrow"), None),
            P(),
            P("narrow", None),
            P(),
            P(None, ("wide", "narrow"), None),
            P(("wide", "narrow"), None, None, None),
            P(("wide", "narrow"), None, None),
        ),
        out_specs=P(None, ("wide", "narrow"), None),
        check_vma=False,
    )
```

profile of v0, /device:TPU:0, one launch (start us, length us, event | category | flops | bytes accessed | tf_op | source)
XLA Modules:
  0.0 638.8 jit_solution(5668109695302431797)
XLA Ops:
  32.3 42.5 %all-to-all-done = bf16[32,256,2,128]{3,1,2,0:T(8,128)(2,1)} async-done(((bf16[32,256,2,128]{3,1,2,0:T(8,128)(2,1)}), bf16[32,256,2,128]{3,1,2,0:T(8,128)(2,1)}, u32[]{:S(2)}, u32[]{:S(2)}) %all-to-all-start) | async-done | bytes 4194336 | tf_op jit(solution)/shard_map/all_to_all | solution.py:78
  85.8 80.3 %while.46 = (s32[]{:T(128)}, f32[128,2,8]{0,2,1:T(8,128)S(1)}, f32[128,2,8]{0,2,1:T(8,128)S(1)}, f32[128,2,8,64]{0,3,2,1:T(8,128)}, s32[4,2048]{1,0:T(4,128)S(1)...) while((s32[]{:T(128)}, f32[128,2,8]{0,2,1:T(8,128)S(1)}, ...), condition=%wide.region_17.18_spmd.clone, body=%wide.region_14.17_spmd.clone.sunk | while | flops 1128667136 | bytes 122046616 | solution.py:149
  96.7 9.1 %fusion.195 = f32[128,2,8,64]{0,3,2,1:T(8,128)} fusion(f32[2,2048,128,8]{2,1,3,0:T(8,128)} %copy-done.1, f32[128,2,8]{0,2,1:T(8,128)S(1)} %max.78, pred[2048]{0:T(1024)(128)(4,1)S(1)} %compare_reduce_fusion.7, bf16[2048,2,128]{0,2,1:T(8,128)(2,1)S(1)} %dynamic-slice_bitcast_fusion.7, f32[128,2,8,64]{0,3,2,1:T(8,128)} %get-tuple-element.681, ...), kind=kOutput, calls=%fused_computation.34.clone.1 | convolution fusion | flops 558235648 | bytes 18370560 | tf_op jit(solution)/shard_map/while/body/eval_jaxpr/rhgk,khe->rhge/dot_general | solution.py:31
  116.6 9.2 %fusion.195 = f32[128,2,8,64]{0,3,2,1:T(8,128)} fusion(f32[2,2048,128,8]{2,1,3,0:T(8,128)} %copy-done.1, f32[128,2,8]{0,2,1:T(8,128)S(1)} %max.78, pred[2048]{0:T(1024)(128)(4,1)S(1)} %compare_reduce_fusion.7, bf16[2048,2,128]{0,2,1:T(8,128)(2,1)S(1)} %dynamic-slice_bitcast_fusion.7, f32[128,2,8,64]{0,3,2,1:T(8,128)} %get-tuple-element.681, ...), kind=kOutput, calls=%fused_computation.34.clone.1 | convolution fusion | flops 558235648 | bytes 18370560 | tf_op jit(solution)/shard_map/while/body/eval_jaxpr/rhgk,khe->rhge/dot_general | solution.py:31
  136.7 9.2 %fusion.195 = f32[128,2,8,64]{0,3,2,1:T(8,128)} fusion(f32[2,2048,128,8]{2,1,3,0:T(8,128)} %copy-done.1, f32[128,2,8]{0,2,1:T(8,128)S(1)} %max.78, pred[2048]{0:T(1024)(128)(4,1)S(1)} %compare_reduce_fusion.7, bf16[2048,2,128]{0,2,1:T(8,128)(2,1)S(1)} %dynamic-slice_bitcast_fusion.7, f32[128,2,8,64]{0,3,2,1:T(8,128)} %get-tuple-element.681, ...), kind=kOutput, calls=%fused_computation.34.clone.1 | convolution fusion | flops 558235648 | bytes 18370560 | tf_op jit(solution)/shard_map/while/body/eval_jaxpr/rhgk,khe->rhge/dot_general | solution.py:31
  156.8 9.2 %fusion.195 = f32[128,2,8,64]{0,3,2,1:T(8,128)} fusion(f32[2,2048,128,8]{2,1,3,0:T(8,128)} %copy-done.1, f32[128,2,8]{0,2,1:T(8,128)S(1)} %max.78, pred[2048]{0:T(1024)(128)(4,1)S(1)} %compare_reduce_fusion.7, bf16[2048,2,128]{0,2,1:T(8,128)(2,1)S(1)} %dynamic-slice_bitcast_fusion.7, f32[128,2,8,64]{0,3,2,1:T(8,128)} %get-tuple-element.681, ...), kind=kOutput, calls=%fused_computation.34.clone.1 | convolution fusion | flops 558235648 | bytes 18370560 | tf_op jit(solution)/shard_map/while/body/eval_jaxpr/rhgk,khe->rhge/dot_general | solution.py:31
  170.5 12.4 %collective-permute-start.6 = (bf16[64,2,8,64]{0,3,2,1:T(8,128)(2,1)}, bf16[64,2,8,64]{0,3,2,1:T(8,128)(2,1)}, u32[]{:S(2)}, u32[]{:S(2)}) collective-permute-start(bf16[64,2,8,64]{0,3,2,1:T(8,128)(2,1)} %select_convert_fusion.1), channel_id=1, source_target_pairs={{0,4},{4,0},{8,12},{12,8},{16,20},{20,16},{24,28},{28,24},{32,36},... | collective-permute-start | bytes 393224 | tf_op jit(solution)/shard_map/ppermute | solution.py:16
  183.0 80.2 %while.45 = (s32[]{:T(128)}, f32[128,2,8]{0,2,1:T(8,128)S(1)}, f32[128,2,8]{0,2,1:T(8,128)S(1)}, f32[128,2,8,64]{0,3,2,1:T(8,128)}, s32[4,2048]{1,0:T(4,128)S(1)...) while((s32[]{:T(128)}, f32[128,2,8]{0,2,1:T(8,128)S(1)}, ...), condition=%wide.region_3.4_spmd.clone, body=%wide.region_0.3_spmd.clone.sunk | while | flops 1128667136 | bytes 126240976 | solution.py:149
  194.0 8.4 %fusion.191 = f32[128,2,8,64]{0,3,2,1:T(8,128)S(1)} fusion(f32[2,2048,128,8]{2,1,3,0:T(8,128)} %copy-done.2, f32[128,2,8]{0,2,1:T(8,128)S(1)} %max.77, pred[2048]{0:T(1024)(128)(4,1)S(1)} %compare_reduce_fusion.6, bf16[2048,2,128]{0,2,1:T(8,128)(2,1)S(1)} %dynamic-slice_bitcast_fusion.6, f32[128,2,8,64]{0,3,2,1:T(8,128)S(1)} %copy-done.23, ...), kind=kOutput, calls=%fused_computation.11.clone.1 | convolution fusion | flops 558235648 | bytes 18370560 | tf_op jit(solution)/shard_map/while/body/eval_jaxpr/rhgk,khe->rhge/dot_general | solution.py:31
  214.0 8.4 %fusion.191 = f32[128,2,8,64]{0,3,2,1:T(8,128)S(1)} fusion(f32[2,2048,128,8]{2,1,3,0:T(8,128)} %copy-done.2, f32[128,2,8]{0,2,1:T(8,128)S(1)} %max.77, pred[2048]{0:T(1024)(128)(4,1)S(1)} %compare_reduce_fusion.6, bf16[2048,2,128]{0,2,1:T(8,128)(2,1)S(1)} %dynamic-slice_bitcast_fusion.6, f32[128,2,8,64]{0,3,2,1:T(8,128)S(1)} %copy-done.23, ...), kind=kOutput, calls=%fused_computation.11.clone.1 | convolution fusion | flops 558235648 | bytes 18370560 | tf_op jit(solution)/shard_map/while/body/eval_jaxpr/rhgk,khe->rhge/dot_general | solution.py:31
  234.1 8.4 %fusion.191 = f32[128,2,8,64]{0,3,2,1:T(8,128)S(1)} fusion(f32[2,2048,128,8]{2,1,3,0:T(8,128)} %copy-done.2, f32[128,2,8]{0,2,1:T(8,128)S(1)} %max.77, pred[2048]{0:T(1024)(128)(4,1)S(1)} %compare_reduce_fusion.6, bf16[2048,2,128]{0,2,1:T(8,128)(2,1)S(1)} %dynamic-slice_bitcast_fusion.6, f32[128,2,8,64]{0,3,2,1:T(8,128)S(1)} %copy-done.23, ...), kind=kOutput, calls=%fused_computation.11.clone.1 | convolution fusion | flops 558235648 | bytes 18370560 | tf_op jit(solution)/shard_map/while/body/eval_jaxpr/rhgk,khe->rhge/dot_general | solution.py:31
  254.1 8.4 %fusion.191 = f32[128,2,8,64]{0,3,2,1:T(8,128)S(1)} fusion(f32[2,2048,128,8]{2,1,3,0:T(8,128)} %copy-done.2, f32[128,2,8]{0,2,1:T(8,128)S(1)} %max.77, pred[2048]{0:T(1024)(128)(4,1)S(1)} %compare_reduce_fusion.6, bf16[2048,2,128]{0,2,1:T(8,128)(2,1)S(1)} %dynamic-slice_bitcast_fusion.6, f32[128,2,8,64]{0,3,2,1:T(8,128)S(1)} %copy-done.23, ...), kind=kOutput, calls=%fused_computation.11.clone.1 | convolution fusion | flops 558235648 | bytes 18370560 | tf_op jit(solution)/shard_map/while/body/eval_jaxpr/rhgk,khe->rhge/dot_general | solution.py:31
  266.6 80.4 %while.47 = (s32[]{:T(128)}, f32[128,2,8]{0,2,1:T(8,128)S(1)}, f32[128,2,8]{0,2,1:T(8,128)S(1)}, f32[128,2,8,64]{0,3,2,1:T(8,128)}, s32[4,2048]{1,0:T(4,128)S(1)...) while((s32[]{:T(128)}, f32[128,2,8]{0,2,1:T(8,128)S(1)}, ...), condition=%wide.region_31.32_spmd.clone, body=%wide.region_28.31_spmd.clone.sunk | while | flops 1128667136 | bytes 122046616 | solution.py:149
  277.5 9.1 %fusion.199 = f32[128,2,8,64]{0,3,2,1:T(8,128)} fusion(f32[2,2048,128,8]{2,1,3,0:T(8,128)} %copy-done.3, f32[128,2,8]{0,2,1:T(8,128)S(1)} %max.79, pred[2048]{0:T(1024)(128)(4,1)S(1)} %compare_reduce_fusion.8, bf16[2048,2,128]{0,2,1:T(8,128)(2,1)S(1)} %dynamic-slice_bitcast_fusion.8, f32[128,2,8,64]{0,3,2,1:T(8,128)} %get-tuple-element.621, ...), kind=kOutput, calls=%fused_computation.57.clone.1 | convolution fusion | flops 558235648 | bytes 18370560 | tf_op jit(solution)/shard_map/while/body/eval_jaxpr/rhgk,khe->rhge/dot_general | solution.py:31
  297.5 9.2 %fusion.199 = f32[128,2,8,64]{0,3,2,1:T(8,128)} fusion(f32[2,2048,128,8]{2,1,3,0:T(8,128)} %copy-done.3, f32[128,2,8]{0,2,1:T(8,128)S(1)} %max.79, pred[2048]{0:T(1024)(128)(4,1)S(1)} %compare_reduce_fusion.8, bf16[2048,2,128]{0,2,1:T(8,128)(2,1)S(1)} %dynamic-slice_bitcast_fusion.8, f32[128,2,8,64]{0,3,2,1:T(8,128)} %get-tuple-element.621, ...), kind=kOutput, calls=%fused_computation.57.clone.1 | convolution fusion | flops 558235648 | bytes 18370560 | tf_op jit(solution)/shard_map/while/body/eval_jaxpr/rhgk,khe->rhge/dot_general | solution.py:31
  317.6 9.3 %fusion.199 = f32[128,2,8,64]{0,3,2,1:T(8,128)} fusion(f32[2,2048,128,8]{2,1,3,0:T(8,128)} %copy-done.3, f32[128,2,8]{0,2,1:T(8,128)S(1)} %max.79, pred[2048]{0:T(1024)(128)(4,1)S(1)} %compare_reduce_fusion.8, bf16[2048,2,128]{0,2,1:T(8,128)(2,1)S(1)} %dynamic-slice_bitcast_fusion.8, f32[128,2,8,64]{0,3,2,1:T(8,128)} %get-tuple-element.621, ...), kind=kOutput, calls=%fused_computation.57.clone.1 | convolution fusion | flops 558235648 | bytes 18370560 | tf_op jit(solution)/shard_map/while/body/eval_jaxpr/rhgk,khe->rhge/dot_general | solution.py:31
  337.7 9.2 %fusion.199 = f32[128,2,8,64]{0,3,2,1:T(8,128)} fusion(f32[2,2048,128,8]{2,1,3,0:T(8,128)} %copy-done.3, f32[128,2,8]{0,2,1:T(8,128)S(1)} %max.79, pred[2048]{0:T(1024)(128)(4,1)S(1)} %compare_reduce_fusion.8, bf16[2048,2,128]{0,2,1:T(8,128)(2,1)S(1)} %dynamic-slice_bitcast_fusion.8, f32[128,2,8,64]{0,3,2,1:T(8,128)} %get-tuple-element.621, ...), kind=kOutput, calls=%fused_computation.57.clone.1 | convolution fusion | flops 558235648 | bytes 18370560 | tf_op jit(solution)/shard_map/while/body/eval_jaxpr/rhgk,khe->rhge/dot_general | solution.py:31
  376.7 23.2 %reduce-scatter.4.cloned.1.call-done = bf16[16,2880]{1,0:T(8,128)(2,1)} async-done(((bf16[64,2880]{1,0:T(8,128)(2,1)}), bf16[16,2880]{1,0:T(8,128)(2,1)}) %reduce-scatter.4.cloned.1.call-update) | async-done | bytes 92176 | tf_op jit(solution)/shard_map/reduce_scatter | solution.py:188
  399.9 23.2 %reduce-scatter.8.cloned.1.call-done = bf16[16,2880]{1,0:T(8,128)(2,1)} async-done(((bf16[64,2880]{1,0:T(8,128)(2,1)}), bf16[16,2880]{1,0:T(8,128)(2,1)}) %reduce-scatter.8.cloned.1.call-update) | async-done | bytes 92176 | tf_op jit(solution)/shard_map/reduce_scatter | solution.py:188
  429.8 8.2 %all-to-all-start.1 = ((bf16[128,2,2880]{2,1,0:T(2,128)(2,1)}), bf16[128,2,2880]{2,1,0:T(2,128)(2,1)S(1)}, u32[]{:S(2)}, u32[]{:S(2)}) async-start(bf16[128,2,2880]{2,1,0:T(2,128)(2,1)} %bitcast.17), calls=%async_computation.2 | async-start | bytes 3014656 | tf_op jit(solution)/shard_map/all_to_all | solution.py:41
  442.1 19.6 %all-to-all-done.1 = bf16[128,2,2880]{2,1,0:T(2,128)(2,1)S(1)} async-done(((bf16[128,2,2880]{2,1,0:T(2,128)(2,1)}), bf16[128,2,2880]{2,1,0:T(2,128)(2,1)S(1)}, u32[]{:S(2)}, u32[]{:S(2)}) %all-to-all-start.1) | async-done | bytes 1474592 | tf_op jit(solution)/shard_map/all_to_all | solution.py:41
  475.7 16.1 %all-to-all-done.3 = bf16[128,2,2880]{2,1,0:T(2,128)(2,1)S(1)} async-done(((bf16[128,2,2880]{2,1,0:T(2,128)(2,1)}), bf16[128,2,2880]{2,1,0:T(2,128)(2,1)S(1)}, u32[]{:S(2)}, u32[]{:S(2)}) %all-to-all-start.3) | async-done | bytes 1474592 | tf_op jit(solution)/shard_map/all_to_all | solution.py:41
  583.2 10.6 %all-to-all-start.6 = ((bf16[128,2,2880]{2,1,0:T(2,128)(2,1)}), bf16[128,2,2880]{2,1,0:T(2,128)(2,1)}, u32[]{:S(2)}, u32[]{:S(2)}) async-start(bf16[128,2,2880]{2,1,0:T(2,128)(2,1)} %copy.211), calls=%async_computation.9 | async-start | bytes 3014656 | tf_op jit(solution)/shard_map/all_to_all | solution.py:45
  605.5 11.6 %all-to-all-done.6 = bf16[128,2,2880]{2,1,0:T(2,128)(2,1)} async-done(((bf16[128,2,2880]{2,1,0:T(2,128)(2,1)}), bf16[128,2,2880]{2,1,0:T(2,128)(2,1)}, u32[]{:S(2)}, u32[]{:S(2)}) %all-to-all-start.6) | async-done | bytes 1474592 | tf_op jit(solution)/shard_map/all_to_all | solution.py:45
  (400 shorter events, 347.0 us)
Async XLA Ops:
  6.5 417.8 %copy-start = (bf16[2880,64]{0,1:T(8,128)(2,1)S(1)}, bf16[2880,64]{0,1:T(8,128)(2,1)}, u32[]{:S(2)}) copy-start(bf16[2880,64]{0,1:T(8,128)(2,1)} %param.26) | copy-start | bytes 1105924
  7.6 19.9 %collective-permute-start = (bf16[64,1024]{1,0:T(8,128)(2,1)S(1)}, bf16[64,1024]{1,0:T(8,128)(2,1)S(1)}, u32[]{:S(2)}, u32[]{:S(2)}) collective-permute-start(bf16[64,1024]{1,0:T(8,128)(2,1)S(1)} %get-tuple-element.418), channel_id=1, source_target_pairs={{0,4},{4,0},{8,12},{12,8},{16,20},{20,16},{24,28},{28,24},{32,36},... | collective-permute-start | bytes 393224 | tf_op jit(solution)/shard_map/ppermute | solution.py:16
  7.7 19.8 %collective-permute-start.4 = (bf16[64,1024]{1,0:T(8,128)(2,1)S(1)}, bf16[64,1024]{1,0:T(8,128)(2,1)S(1)}, u32[]{:S(2)}, u32[]{:S(2)}) collective-permute-start(bf16[64,1024]{1,0:T(8,128)(2,1)S(1)} %get-tuple-element.417), channel_id=1, source_target_pairs={{0,4},{4,0},{8,12},{12,8},{16,20},{20,16},{24,28},{28,24},{32,36},... | collective-permute-start | bytes 393224 | tf_op jit(solution)/shard_map/ppermute | solution.py:16
  8.2 19.3 %collective-permute-start.8 = (bf16[64,1024]{1,0:T(8,128)(2,1)S(1)}, bf16[64,1024]{1,0:T(8,128)(2,1)S(1)}, u32[]{:S(2)}, u32[]{:S(2)}) collective-permute-start(bf16[64,1024]{1,0:T(8,128)(2,1)S(1)} %get-tuple-element.419), channel_id=1, source_target_pairs={{0,4},{4,0},{8,12},{12,8},{16,20},{20,16},{24,28},{28,24},{32,36},... | collective-permute-start | bytes 393224 | tf_op jit(solution)/shard_map/ppermute | solution.py:16
  13.6 61.2 %all-to-all-start = ((bf16[32,256,2,128]{3,1,2,0:T(8,128)(2,1)}), bf16[32,256,2,128]{3,1,2,0:T(8,128)(2,1)}, u32[]{:S(2)}, u32[]{:S(2)}) async-start(bf16[32,256,2,128]{3,1,2,0:T(8,128)(2,1)} %copy.177), calls=%async_computation | async-start | bytes 8388608 | tf_op jit(solution)/shard_map/all_to_all | solution.py:78
  21.3 355.4 %reduce-scatter.6.cloned.1.call-start = ((), (), s32[]{:S(2)}) async-start(), calls=%async_computation.11 | async-start | bytes 471040 | tf_op jit(solution)/shard_map/reduce_scatter | solution.py:188
  167.7 181.5 %collective-permute-start.7 = (bf16[64,2,8]{0,2,1:T(8,128)(2,1)}, bf16[64,2,8]{0,2,1:T(8,128)(2,1)}, u32[]{:S(2)}, u32[]{:S(2)}) collective-permute-start(bf16[64,2,8]{0,2,1:T(8,128)(2,1)} %select_convert_fusion.5), channel_id=1, source_target_pairs={{0,4},{4,0},{8,12},{12,8},{16,20},{20,16},{24,28},{28,24},{32,36},... | collective-permute-start | bytes 6152 | tf_op jit(solution)/shard_map/ppermute | solution.py:16
  167.7 182.0 %collective-permute-start.5 = (bf16[64,2,8]{0,2,1:T(8,128)(2,1)}, bf16[64,2,8]{0,2,1:T(8,128)(2,1)}, u32[]{:S(2)}, u32[]{:S(2)}) collective-permute-start(bf16[64,2,8]{0,2,1:T(8,128)(2,1)} %select_convert_fusion.6), channel_id=1, source_target_pairs={{0,4},{4,0},{8,12},{12,8},{16,20},{20,16},{24,28},{28,24},{32,36},... | collective-permute-start | bytes 6152 | tf_op jit(solution)/shard_map/ppermute | solution.py:16
  170.5 180.0 %collective-permute-start.6 = (bf16[64,2,8,64]{0,3,2,1:T(8,128)(2,1)}, bf16[64,2,8,64]{0,3,2,1:T(8,128)(2,1)}, u32[]{:S(2)}, u32[]{:S(2)}) collective-permute-start(bf16[64,2,8,64]{0,3,2,1:T(8,128)(2,1)} %select_convert_fusion.1), channel_id=1, source_target_pairs={{0,4},{4,0},{8,12},{12,8},{16,20},{20,16},{24,28},{28,24},{32,36},... | collective-permute-start | bytes 393224 | tf_op jit(solution)/shard_map/ppermute | solution.py:16
  183.0 83.5 %copy-start.5 = (bf16[128,1024]{0,1:T(8,128)(2,1)S(1)}, bf16[128,1024]{0,1:T(8,128)(2,1)}, u32[]{:S(2)}) copy-start(bf16[128,1024]{0,1:T(8,128)(2,1)} %copy-done.4) | copy-start | bytes 786436
  263.5 94.0 %collective-permute-start.3 = (bf16[64,2,8]{0,2,1:T(8,128)(2,1)S(1)}, bf16[64,2,8]{0,2,1:T(8,128)(2,1)S(1)}, u32[]{:S(2)}, u32[]{:S(2)}) collective-permute-start(bf16[64,2,8]{0,2,1:T(8,128)(2,1)S(1)} %select_convert_fusion.7), channel_id=1, source_target_pairs={{0,4},{4,0},{8,12},{12,8},{16,20},{20,16},{24,28},{28,24},{32,36},... | collective-permute-start | bytes 6152 | tf_op jit(solution)/shard_map/ppermute | solution.py:16
  264.1 93.7 %collective-permute-start.1 = (bf16[64,2,8]{0,2,1:T(8,128)(2,1)S(1)}, bf16[64,2,8]{0,2,1:T(8,128)(2,1)S(1)}, u32[]{:S(2)}, u32[]{:S(2)}) collective-permute-start(bf16[64,2,8]{0,2,1:T(8,128)(2,1)S(1)} %select_convert_fusion.8), channel_id=1, source_target_pairs={{0,4},{4,0},{8,12},{12,8},{16,20},{20,16},{24,28},{28,24},{32,36},... | collective-permute-start | bytes 6152 | tf_op jit(solution)/shard_map/ppermute | solution.py:16
  349.2 8.7 %collective-permute-start.2 = (bf16[64,2,8,64]{0,3,2,1:T(8,128)(2,1)S(1)}, bf16[64,2,8,64]{0,3,2,1:T(8,128)(2,1)S(1)}, u32[]{:S(2)}, u32[]{:S(2)}) collective-permute-start(bf16[64,2,8,64]{0,3,2,1:T(8,128)(2,1)S(1)} %copy-done.31), channel_id=1, source_target_pairs={{0,4},{4,0},{8,12},{12,8},{16,20},{20,16},{24,28},{28,24},{32,36},... | collective-permute-start | bytes 393224 | tf_op jit(solution)/shard_map/ppermute | solution.py:16
  349.6 14.2 %collective-permute-start.11 = (bf16[64,2,8]{0,2,1:T(8,128)(2,1)S(1)}, bf16[64,2,8]{0,2,1:T(8,128)(2,1)S(1)}, u32[]{:S(2)}, u32[]{:S(2)}) collective-permute-start(bf16[64,2,8]{0,2,1:T(8,128)(2,1)S(1)} %select_convert_fusion.3), channel_id=1, source_target_pairs={{0,4},{4,0},{8,12},{12,8},{16,20},{20,16},{24,28},{28,24},{32,36},... | collective-permute-start | bytes 6152 | tf_op jit(solution)/shard_map/ppermute | solution.py:16
  350.5 13.3 %collective-permute-start.9 = (bf16[64,2,8]{0,2,1:T(8,128)(2,1)S(1)}, bf16[64,2,8]{0,2,1:T(8,128)(2,1)S(1)}, u32[]{:S(2)}, u32[]{:S(2)}) collective-permute-start(bf16[64,2,8]{0,2,1:T(8,128)(2,1)S(1)} %select_convert_fusion.4), channel_id=1, source_target_pairs={{0,4},{4,0},{8,12},{12,8},{16,20},{20,16},{24,28},{28,24},{32,36},... | collective-permute-start | bytes 6152 | tf_op jit(solution)/shard_map/ppermute | solution.py:16
  357.5 42.4 %reduce-scatter.4.cloned.1.call-start = ((), (), s32[]{:S(2)}) async-start(), calls=%async_computation.10 | async-start | bytes 471040 | tf_op jit(solution)/shard_map/reduce_scatter | solution.py:188
  357.6 6.3 collective-permute-start.10
  363.4 59.7 %reduce-scatter.8.cloned.1.call-start = ((), (), s32[]{:S(2)}) async-start(), calls=%async_computation.12 | async-start | bytes 471040 | tf_op jit(solution)/shard_map/reduce_scatter | solution.py:188
  429.8 31.8 %all-to-all-start.1 = ((bf16[128,2,2880]{2,1,0:T(2,128)(2,1)}), bf16[128,2,2880]{2,1,0:T(2,128)(2,1)S(1)}, u32[]{:S(2)}, u32[]{:S(2)}) async-start(bf16[128,2,2880]{2,1,0:T(2,128)(2,1)} %bitcast.17), calls=%async_computation.2 | async-start | bytes 3014656 | tf_op jit(solution)/shard_map/all_to_all | solution.py:41
  463.6 28.2 %all-to-all-start.3 = ((bf16[128,2,2880]{2,1,0:T(2,128)(2,1)}), bf16[128,2,2880]{2,1,0:T(2,128)(2,1)S(1)}, u32[]{:S(2)}, u32[]{:S(2)}) async-start(bf16[128,2,2880]{2,1,0:T(2,128)(2,1)} %bitcast.359), calls=%async_computation.5 | async-start | bytes 3014656 | tf_op jit(solution)/shard_map/all_to_all | solution.py:41
  494.8 29.1 %all-to-all-start.5 = ((bf16[128,2,2880]{2,1,0:T(2,128)(2,1)}), bf16[128,2,2880]{2,1,0:T(2,128)(2,1)}, u32[]{:S(2)}, u32[]{:S(2)}) async-start(bf16[128,2,2880]{2,1,0:T(2,128)(2,1)} %bitcast.360), calls=%async_computation.8 | async-start | bytes 3014656 | tf_op jit(solution)/shard_map/all_to_all | solution.py:41
  523.9 28.2 %all-to-all-start.2 = ((bf16[128,2,2880]{2,1,0:T(2,128)(2,1)}), bf16[128,2,2880]{2,1,0:T(2,128)(2,1)S(1)}, u32[]{:S(2)}, u32[]{:S(2)}) async-start(bf16[128,2,2880]{2,1,0:T(2,128)(2,1)} %copy.188), calls=%async_computation.3 | async-start | bytes 3014656 | tf_op jit(solution)/shard_map/all_to_all | solution.py:45
  552.2 31.0 %all-to-all-start.4 = ((bf16[128,2,2880]{2,1,0:T(2,128)(2,1)}), bf16[128,2,2880]{2,1,0:T(2,128)(2,1)S(1)}, u32[]{:S(2)}, u32[]{:S(2)}) async-start(bf16[128,2,2880]{2,1,0:T(2,128)(2,1)} %copy.200), calls=%async_computation.6 | async-start | bytes 3014656 | tf_op jit(solution)/shard_map/all_to_all | solution.py:45
  583.2 33.8 %all-to-all-start.6 = ((bf16[128,2,2880]{2,1,0:T(2,128)(2,1)}), bf16[128,2,2880]{2,1,0:T(2,128)(2,1)}, u32[]{:S(2)}, u32[]{:S(2)}) async-start(bf16[128,2,2880]{2,1,0:T(2,128)(2,1)} %copy.211), calls=%async_computation.9 | async-start | bytes 3014656 | tf_op jit(solution)/shard_map/all_to_all | solution.py:45
  (57 other events, 1127.8 us)
Sparse Core Ops, SparseCore 0:
  357.6 19.0 reduce-scatter.5
  379.2 20.6 reduce-scatter.3
  402.3 20.7 reduce-scatter.7
where the time goes:
time: 651 us; the launch traced here: 639 us
  matrix products  214 us (33%)
  waiting for transfers between devices  153 us (24%)
  local copies, waits for them, and re-layouts  98.7 us (15%)
  other arithmetic  93 us (14%)
  starting transfers between devices  62.8 us (10%)
  between operations  16.6 us (3%)
    dot_general x15, matrix products, absorb(): jnp.einsum('rhgk,khe->rhge', weights.astype(jnp.bfloat16), value_rows, pr...  111 us
    reduce_sum x15, other arithmetic, absorb(): new_total = old_total * rescale + jnp.sum(weights, axis=-1)  59.2 us
    reduce_scatter x3, waiting for transfers between devices, shards(): lax.psum_scatter(jnp.dot(attended, w_out, preferred_element_type=jnp.floa...  52.1 us
    all_to_all x1, waiting for transfers between devices, shards(): lax.all_to_all(pieces, 'wide', split_axis=0, concat_axis=0, tiled=True)  42.5 us
    dot_general x15, matrix products, absorb(): jnp.einsum('rhge,khe->rhgk', both_q, key_rows, preferred_element_type=jnp...  41.9 us
    all_to_all x3, waiting for transfers between devices, send_rows(): lax.all_to_all(outgoing, ('wide', 'narrow'), split_axis=0, concat_axis=0,...  41.7 us
    all_to_all x3, starting transfers between devices, send_back(): lax.all_to_all(results.astype(jnp.bfloat16), ('wide', 'narrow'), split_ax...  20.4 us
    dot_general x3, matrix products, shards(): jnp.dot(rows_in, gate_up_local, preferred_element_type=jnp.float32)  19.1 us
  transfers between devices with their start and end apart: 22, of which 9 were waited for; matrix products, arithmetic and copies ran while one was open for 43% of the time, Pallas kernels for 0%

commit v1 on v0

v1 whole, which is shorter than its diff:
```python
import functools

import jax
import jax.numpy as jnp
from jax import lax
from jax.experimental import pallas as pl
from jax.experimental.pallas import tpu as pltpu
from jax.sharding import Mesh, PartitionSpec as P

GROUPS = ((0, 1), (2,))
WIDE = ("chip", "core")
ALL = ("chip", "core", "z")
BF16 = jnp.bfloat16
F32 = jnp.float32
HEAD = 64
LANES = 128
NEG = -1e30
LIMIT = 1e30


def partner(block):
    return lax.ppermute(block, "core", [(0, 1), (1, 0)])


def from_ahead(block, distance):
    count = lax.axis_size("z")
    return lax.ppermute(block, "z", [(i, (i - distance) % count) for i in range(count)])


def swap_shards(block):
    depth = lax.axis_size("z")
    route = []
    for z in range(0, depth, 2):
        route += [(depth + z, z + 1), (z + 1, depth + z)]
    return lax.ppermute(block, ("core", "z"), route)


def tie(*arrays):
    return lax.optimization_barrier(arrays)


def round_up(size, unit):
    return -(-size // unit) * unit


def exchange(block, axis):
    return lax.all_to_all(block, axis, split_axis=0, concat_axis=0, tiled=True)


def lane_ids(shape):
    return lax.broadcasted_iota(jnp.int32, shape, len(shape) - 1)


def valid_rows(length, span, core):
    return (length // (2 * span)) * span + jnp.clip(length % (2 * span) - core * span, 0, span)


def fill_queries(q_ref, qs_ref, rows, groups):
    lane = lane_ids((rows, LANES))
    extra = jnp.where(lane == HEAD, 1.0, 0.0)
    for pair in range(groups // 2):
        both = q_ref[:, pair * LANES : (pair + 1) * LANES].astype(F32) * 0.125
        for side in range(2):
            group = 2 * pair + side
            part = both if side == 0 else pltpu.roll(both, HEAD, 1)
            qs_ref[group * rows : (group + 1) * rows, :] = jnp.where(
                lane < HEAD, part, extra
            ).astype(BF16)


def key_value_rows(block, first, valid):
    shape = block.shape
    lane = lane_ids(shape)
    position = lax.broadcasted_iota(jnp.int32, shape, 0) + first
    bias = jnp.where(position < valid, 0.0, NEG).astype(BF16)
    keys = jnp.where(lane == HEAD, bias, block)
    values = jnp.where(lane < HEAD, jnp.ones_like(block), block)
    return keys, values


def score(query_rows, keys):
    return lax.dot_general(query_rows, keys, (((1,), (1,)), ((), ())), preferred_element_type=F32)


def add_chunk(qs_ref, kv_ref, acc_ref, valid, total_rows, query_span, key_span):
    def key_block(index, carry):
        first = pl.multiple_of(index * key_span, key_span)
        keys, values = key_value_rows(kv_ref[pl.ds(first, key_span), :], first, valid)

        def query_block(number, inner):
            at = pl.ds(pl.multiple_of(number * query_span, query_span), query_span)
            weights = jnp.exp(score(qs_ref[at, :], keys)).astype(BF16)
            acc_ref[at, :] += jnp.dot(weights, values, preferred_element_type=F32)
            return inner

        return lax.fori_loop(0, total_rows // query_span, query_block, carry)

    lax.fori_loop(0, (valid + key_span - 1) // key_span, key_block, 0)


def safe_update(scores, values, at, acc_ref, peak_ref):
    old = peak_ref[at, :]
    new = jnp.maximum(old, jnp.max(scores, axis=1, keepdims=True))
    weights = jnp.exp(scores - new[:, :1]).astype(BF16)
    acc_ref[at, :] = acc_ref[at, :] * jnp.exp(old - new) + jnp.dot(
        weights, values, preferred_element_type=F32
    )
    peak_ref[at, :] = new


def first_kernel(span, groups, query_span, key_span, at_ref, q_ref, kv_ref, acc_ref, qs_ref):
    rows = q_ref.shape[0]
    fill_queries(q_ref, qs_ref, rows, groups)
    acc_ref[...] = jnp.zeros_like(acc_ref)
    valid = valid_rows(at_ref[0], span, at_ref[1])
    add_chunk(qs_ref, kv_ref, acc_ref, valid, rows * groups, query_span, key_span)


def last_kernel(
    span,
    groups,
    first_row,
    query_span,
    key_span,
    at_ref,
    sink_ref,
    q_ref,
    recent_ref,
    kv_near_ref,
    kv_far_ref,
    acc_in_ref,
    out_ref,
    acc_ref,
    qs_ref,
    peak_ref,
):
    rows = q_ref.shape[0]
    recents = recent_ref.shape[0]
    total = rows * groups
    fill_queries(q_ref, qs_ref, rows, groups)
    recent_keys, recent_values = key_value_rows(recent_ref[...], 0, recents)
    row_id = lax.broadcasted_iota(jnp.int32, (rows, recents), 0) + first_row
    causal = lane_ids((rows, recents)) <= row_id

    def recent_scores(group):
        at = pl.ds(group * rows, rows)
        return jnp.where(causal, score(qs_ref[at, :], recent_keys), NEG)

    for group in range(groups):
        at = pl.ds(group * rows, rows)
        weights = jnp.exp(recent_scores(group)).astype(BF16)
        gained = jnp.dot(weights, recent_values, preferred_element_type=F32)
        acc_ref[at, :] = acc_in_ref[at, :] + gained
    near = valid_rows(at_ref[0], span, at_ref[1])
    far = valid_rows(at_ref[0], span, 1 - at_ref[1])
    add_chunk(qs_ref, kv_far_ref, acc_ref, far, total, query_span, key_span)
    lane = lane_ids((rows, LANES))

    def finish(shifted):
        for pair in range(groups // 2):
            halves = []
            for side in range(2):
                group = 2 * pair + side
                at = pl.ds(group * rows, rows)
                sink = jnp.full((rows, LANES), sink_ref[group], F32)
                own = jnp.exp(sink - peak_ref[at, :]) if shifted else jnp.exp(sink)
                value = acc_ref[at, :]
                if side == 0:
                    halves.append(pltpu.roll(value, HEAD, 1) / (value + own))
                else:
                    halves.append(value / (pltpu.roll(value, HEAD, 1) + own))
            out_ref[:, pair * LANES : (pair + 1) * LANES] = jnp.where(
                lane < HEAD, halves[0], halves[1]
            ).astype(BF16)

    acc_lane = lane_ids((total, LANES))
    weight_sums = jnp.where(acc_lane < HEAD, acc_ref[...], 0.0)
    fits = jnp.max(jnp.where(weight_sums < LIMIT, 0.0, 1.0)) == 0.0

    @pl.when(fits)
    def plain():
        finish(False)

    @pl.when(jnp.logical_not(fits))
    def careful():
        acc_ref[...] = jnp.zeros_like(acc_ref)
        for group in range(groups):
            at = pl.ds(group * rows, rows)
            peak_ref[at, :] = jnp.full((rows, LANES), sink_ref[group], F32)
            safe_update(recent_scores(group), recent_values, at, acc_ref, peak_ref)
        block = 256
        for kv_ref, limit in ((kv_near_ref, near), (kv_far_ref, far)):

            def key_block(index, carry, kv_ref=kv_ref, limit=limit):
                first = pl.multiple_of(index * block, block)
                keys, values = key_value_rows(kv_ref[pl.ds(first, block), :], first, limit)

                def query_block(number, inner):
                    at = pl.ds(pl.multiple_of(number * block, block), block)
                    safe_update(score(qs_ref[at, :], keys), values, at, acc_ref, peak_ref)
                    return inner

                return lax.fori_loop(0, total // block, query_block, carry)

            lax.fori_loop(0, (limit + block - 1) // block, key_block, 0)
        finish(True)


SMEM_SPEC = pl.BlockSpec(memory_space=pltpu.SMEM)
VMEM_SPEC = pl.BlockSpec(memory_space=pltpu.VMEM)
ATTEND = pltpu.CompilerParams(vmem_limit_bytes=30 * 2**20)
EXPERT = pltpu.CompilerParams(vmem_limit_bytes=40 * 2**20)
SMALL = pltpu.CompilerParams(vmem_limit_bytes=16 * 2**20)


def attention_cost(rows, groups, keys):
    return pl.CostEstimate(
        flops=8 * rows * groups * keys * LANES,
        bytes_accessed=keys * LANES * 2,
        transcendentals=rows * groups * keys,
    )


def attend_first(place, q, kv, span, groups):
    rows = q.shape[0]
    total = rows * groups
    return pl.pallas_call(
        functools.partial(first_kernel, span, groups, 1024, 2048),
        out_shape=jax.ShapeDtypeStruct((total, LANES), F32),
        in_specs=[SMEM_SPEC, VMEM_SPEC, VMEM_SPEC],
        out_specs=VMEM_SPEC,
        scratch_shapes=[pltpu.VMEM((total, LANES), BF16)],
        compiler_params=ATTEND,
        cost_estimate=attention_cost(rows, groups, kv.shape[0]),
        name="attend_first",
    )(place, q, kv)


def attend_last(place, sink, q, recent, near, far, acc, span, groups, first_row):
    rows, width = q.shape
    total = rows * groups
    return pl.pallas_call(
        functools.partial(last_kernel, span, groups, first_row, 1024, 2048),
        out_shape=jax.ShapeDtypeStruct((rows, width), BF16),
        in_specs=[SMEM_SPEC, SMEM_SPEC] + [VMEM_SPEC] * 5,
        out_specs=VMEM_SPEC,
        scratch_shapes=[
            pltpu.VMEM((total, LANES), F32),
            pltpu.VMEM((total, LANES), BF16),
            pltpu.VMEM((total, LANES), F32),
        ],
        compiler_params=ATTEND,
        cost_estimate=attention_cost(rows, groups, far.shape[0]),
        name="attend_last",
    )(place, sink, q, recent, near, far, acc)


def split_kernel(side_ref, rows_ref, near_ref, far_ref):
    tile = 256
    half = tile // 2
    row = lax.broadcasted_iota(jnp.int32, (tile, tile), 0)
    column = lax.broadcasted_iota(jnp.int32, (tile, tile), 1)
    side = jnp.where(row < half, side_ref[0], 1 - side_ref[0])
    source = 2 * (row % half) + side
    chooser = jnp.where(column == source, 1.0, 0.0).astype(BF16)
    for index in range(rows_ref.shape[0] // tile):
        block = rows_ref[index * tile : (index + 1) * tile, :]
        chosen = jnp.dot(chooser, block, preferred_element_type=F32).astype(BF16)
        near_ref[index * half : (index + 1) * half, :] = chosen[:half]
        far_ref[index * half : (index + 1) * half, :] = chosen[half:]


def split_heads(side, cache):
    requests, span, kv_local, packed = cache.shape
    rows = requests * span
    tile = rows // 8
    near, far = pl.pallas_call(
        split_kernel,
        grid=(8,),
        out_shape=(jax.ShapeDtypeStruct((rows, packed), BF16),) * 2,
        in_specs=[SMEM_SPEC, pl.BlockSpec((kv_local * tile, packed), lambda i: (i, 0))],
        out_specs=(pl.BlockSpec((tile, packed), lambda i: (i, 0)),) * 2,
        compiler_params=SMALL,
        name="split_heads",
    )(side.astype(jnp.int32)[None], cache.reshape(rows * kv_local, packed))
    shape = (requests, span, packed)
    return near.reshape(shape), far.reshape(shape)


def pack_kernel(slot_ref, rows_ref, out_ref):
    rows = rows_ref.shape[0]
    tile = 128
    for first in range(0, out_ref.shape[0], tile):
        place = lax.broadcasted_iota(jnp.int32, (tile, rows), 0) + first
        hit = slot_ref[0:1, :] == place
        for k in range(1, slot_ref.shape[0]):
            hit = jnp.logical_or(hit, slot_ref[k : k + 1, :] == place)
        chooser = jnp.where(hit, 1.0, 0.0).astype(BF16)
        out_ref[first : first + tile, :] = jnp.dot(
            chooser, rows_ref[...], preferred_element_type=F32
        ).astype(BF16)


def pack_rows(slot, rows, slots):
    return pl.pallas_call(
        pack_kernel,
        out_shape=jax.ShapeDtypeStruct((slots, rows.shape[1]), BF16),
        in_specs=[VMEM_SPEC] * 2,
        out_specs=VMEM_SPEC,
        compiler_params=SMALL,
        cost_estimate=pl.CostEstimate(
            flops=2 * slots * rows.size, bytes_accessed=4 * slots * rows.shape[1], transcendentals=0
        ),
        name="pack_rows",
    )(slot, rows)


def expert_kernel(own_ref, other_ref, gate_up_ref, down_ref, own_out_ref, other_out_ref):
    tile = 256
    width = down_ref.shape[1]
    for rows_ref, out_ref in ((own_ref, own_out_ref), (other_ref, other_out_ref)):

        def step(index, carry, rows_ref=rows_ref, out_ref=out_ref):
            at = pl.ds(pl.multiple_of(index * tile, tile), tile)
            rows = rows_ref[at, :width]
            gate_part = jnp.minimum(jnp.dot(rows, gate_up_ref[0], preferred_element_type=F32), 7.0)
            up_part = jnp.clip(
                jnp.dot(rows, gate_up_ref[1], preferred_element_type=F32), -7.0, 7.0
            )
            activation = gate_part * jax.nn.sigmoid(1.702 * gate_part) * (up_part + 1.0)
            result = jnp.dot(activation.astype(BF16), down_ref[...], preferred_element_type=F32)
            out_ref[at, :width] = result.astype(BF16)
            out_ref[at, width:] = jnp.zeros((tile, out_ref.shape[1] - width), BF16)
            return carry

        lax.fori_loop(0, rows_ref.shape[0] // tile, step, 0)


def expert_rows(own, other, gate_up, down):
    return pl.pallas_call(
        expert_kernel,
        out_shape=(jax.ShapeDtypeStruct(own.shape, BF16),) * 2,
        in_specs=[VMEM_SPEC] * 4,
        out_specs=(VMEM_SPEC, VMEM_SPEC),
        compiler_params=EXPERT,
        cost_estimate=pl.CostEstimate(
            flops=4 * own.shape[0] * (gate_up.size + down.size),
            bytes_accessed=2 * (gate_up.size + down.size + 4 * own.size),
            transcendentals=2 * own.shape[0] * down.shape[0],
        ),
        name="expert_rows",
    )(own, other, gate_up, down)


def blend_kernel(slot_ref, gate_ref, back_ref, out_ref):
    rows = slot_ref.shape[0]
    place = lane_ids((rows, back_ref.shape[0]))
    blender = jnp.zeros(place.shape, F32)
    for k in range(slot_ref.shape[1]):
        blender += jnp.where(slot_ref[:, k : k + 1] == place, gate_ref[:, k : k + 1], 0.0)
    high = blender.astype(BF16)
    low = (blender - high.astype(F32)).astype(BF16)
    both = jnp.concatenate([high, low], axis=0)
    mixed = jnp.dot(both, back_ref[...], preferred_element_type=F32)
    out_ref[...] = mixed[:rows] + mixed[rows:]


def blend_rows(slot, gates, back):
    rows = slot.shape[0]
    return pl.pallas_call(
        blend_kernel,
        out_shape=jax.ShapeDtypeStruct((rows, back.shape[1]), F32),
        in_specs=[VMEM_SPEC] * 3,
        out_specs=VMEM_SPEC,
        compiler_params=SMALL,
        cost_estimate=pl.CostEstimate(
            flops=4 * rows * back.size, bytes_accessed=2 * back.size, transcendentals=0
        ),
        name="blend_rows",
    )(slot, gates, back)


def shards(
    cache,
    lengths,
    queries,
    new_kv,
    sinks,
    residual,
    norm_gain,
    w_out,
    w_router,
    expert_ids,
    w_gate_up,
    w_down,
):
    depth = lax.axis_size("z")
    side = lax.axis_index("core")
    z_index = lax.axis_index("z")
    request = lax.axis_index("chip")
    requests, span, kv_local, packed = cache.shape
    steps, own_rows, q_width = queries.shape
    head_width = q_width // kv_local
    groups = head_width // HEAD
    rows_req = 2 * own_rows
    rows_dev = own_rows // depth
    model_dim = residual.shape[2]
    experts = w_router.shape[1]
    top_k = expert_ids.shape[2]
    capacity = rows_dev * top_k * 2 // experts
    assigned = rows_dev * top_k
    first_side = side == 0

    near_out, far_out = split_heads(side, cache)
    far_out = partner(far_out)
    near = exchange(near_out, "chip").reshape(requests * span, packed)
    far = exchange(far_out, "chip").reshape(requests * span, packed)

    local = jnp.concatenate(
        [queries.reshape(steps, own_rows, kv_local, head_width), new_kv], axis=3
    )
    keep = jnp.where(first_side, local[:, :, 0], local[:, :, 1])
    got = partner(jnp.where(first_side, local[:, :, 1], local[:, :, 0]))
    joined = jnp.concatenate(
        [jnp.where(first_side, keep, got), jnp.where(first_side, got, keep)], axis=1
    )
    q_all = joined[:, :, :head_width]
    recent = joined[:, :, head_width:].reshape(steps * rows_req, packed)
    place = jnp.concatenate(
        [lax.dynamic_slice_in_dim(lengths, request, 1, 0), side.astype(jnp.int32)[None]]
    )
    sink = lax.dynamic_slice_in_dim(sinks, (z_index * kv_local + side) * groups, groups, 0)

    gain_wide = norm_gain.astype(F32)
    swapped = side != z_index % 2
    far_gate_up = swap_shards(w_gate_up)
    far_down = swap_shards(w_down)
    near, near_gate_up = tie(near, jnp.transpose(w_gate_up[0], (1, 0, 2)))
    padded = round_up(model_dim, LANES)
    ids = expert_ids.reshape(steps, assigned)
    earlier = jnp.arange(assigned)[:, None] > jnp.arange(assigned)[None, :]
    same = ids[..., :, None] == ids[..., None, :]
    rank = jnp.sum((same & earlier).astype(jnp.int32), axis=-1)
    stride = round_up(steps * capacity, 8)
    kind = ids % 4
    target = (ids // 4) * depth + 2 * (kind % 2) + kind // 2
    step_ids = jnp.arange(steps, dtype=jnp.int32)[:, None]
    slot = (target * stride + step_ids * capacity + rank).reshape(steps * rows_dev, top_k)
    ids = ids.reshape(steps * rows_dev, top_k)
    slots = experts * stride
    expert_range = jnp.arange(experts, dtype=jnp.int32)

    def span_of(group, array, axis=0):
        return lax.slice_in_dim(array, group[0], group[-1] + 1, axis=axis)

    def queries_of(group):
        return span_of(group, q_all).reshape(len(group) * rows_req, head_width)

    def finish(group, q, acc):
        return attend_last(
            place, sink, q, recent, near, far, acc, span, groups, group[0] * rows_req
        )

    def project(group, out):
        count = len(group)
        out = out.reshape(count, 2, own_rows, head_width)
        mine = jnp.where(first_side, out[:, 0], out[:, 1])
        theirs = partner(jnp.where(first_side, out[:, 1], out[:, 0]))
        attended = jnp.concatenate(
            [jnp.where(first_side, mine, theirs), jnp.where(first_side, theirs, mine)], axis=2
        )
        attended = jnp.transpose(
            attended.reshape(count, depth, rows_dev, q_width), (1, 0, 2, 3)
        ).reshape(depth * count * rows_dev, q_width)
        part = jnp.dot(attended, w_out, preferred_element_type=F32).astype(BF16)
        return part.reshape(depth, count * rows_dev, model_dim)

    def spread(parts):
        pieces = [lax.dynamic_index_in_dim(parts, z_index, 0, keepdims=False)]
        for distance in range(1, depth):
            piece = lax.dynamic_index_in_dim(
                parts, (z_index - distance) % depth, 0, keepdims=False
            )
            pieces.append(from_ahead(piece, distance))
        return pieces

    def residual_sum(group, pieces):
        base = span_of(group, residual).reshape(len(group) * rows_dev, model_dim)
        return base.astype(F32) + sum(piece.astype(F32) for piece in pieces)

    def normalize(hidden):
        normed = (
            hidden * lax.rsqrt(jnp.mean(hidden * hidden, axis=-1, keepdims=True) + 1e-05) * gain_wide
        ).astype(BF16)
        return jnp.pad(normed, ((0, 0), (0, padded - model_dim)))

    def gates_of(ids, rows):
        logits = jnp.dot(rows[:, :model_dim], w_router, preferred_element_type=F32)
        picked = ids[..., None] == expert_range
        chosen = jnp.sum(jnp.where(picked, logits[:, None, :], 0.0), axis=-1)
        gates = jnp.exp(chosen)
        return gates / jnp.sum(gates, axis=-1, keepdims=True)

    early, late = GROUPS
    q_early, q_late = queries_of(early), queries_of(late)
    acc_early = attend_first(place, q_early, near, span, groups)
    acc_early, q_late = tie(acc_early, q_late)
    acc_late = attend_first(place, q_late, near, span, groups)
    acc_late, acc_early = tie(acc_late, acc_early)
    parts_early = project(early, finish(early, q_early, acc_early))
    parts_early, acc_late = tie(parts_early, acc_late)
    pieces_early = spread(parts_early)
    out_late = finish(late, q_late, acc_late)
    parts_late = project(late, out_late)
    *pieces_early, parts_late = tie(*pieces_early, parts_late)
    pieces = pieces_early + spread(parts_late)
    hidden = jnp.concatenate(
        [residual_sum(early, pieces[:depth]), residual_sum(late, pieces[depth:])]
    )
    rows = normalize(hidden)
    sent = pack_rows(jnp.transpose(slot), rows, slots)
    sent, far_gate_up, far_down, rows = tie(sent, far_gate_up, far_down, rows)
    arrived = exchange(sent.reshape(experts, stride, padded), ("chip", "z"))
    far_gate_up = jnp.transpose(far_gate_up[0], (1, 0, 2))
    gate_up = jnp.where(swapped, far_gate_up, near_gate_up)
    down = jnp.where(swapped, far_down, w_down)[0]
    gates = gates_of(ids, rows)
    arrived, gate_up, down, gates = tie(arrived, gate_up, down, gates)
    arrived = arrived.reshape(slots, padded)
    own, other = expert_rows(arrived, partner(arrived), gate_up, down)
    done = (own.astype(F32) + partner(other).astype(F32)).astype(BF16)
    returned = exchange(done.reshape(experts, stride, padded), ("chip", "z"))
    mixed = blend_rows(slot, gates, returned.reshape(slots, padded))
    out = (hidden + mixed[:, :model_dim]).astype(BF16)
    return out.reshape(steps, rows_dev, model_dim)


def solution(mesh):
    wide = mesh.shape["wide"]
    fine = Mesh(mesh.devices.reshape(wide // 2, 2, mesh.shape["narrow"]), ALL)
    return jax.shard_map(
        shards,
        mesh=fine,
        in_specs=(
            P(None, WIDE, "z", None),
            P(),
            P(None, WIDE, "z"),
            P(None, WIDE, "z", None),
            P(),
            P(None, ALL, None),
            P(),
            P("z", None),
            P(),
            P(None, ALL, None),
            P(ALL, None, None, None),
            P(ALL, None, None),
        ),
        out_specs=P(None, ALL, None),
        check_vma=False,
    )
```

time: 651 us -> 742 us (1.14)
  Pallas kernels: 0 us -> 459 us
  matrix products: 214 us -> 11.1 us
  waiting for transfers between devices: 153 us -> 40.4 us
  other arithmetic: 93 us -> 16 us
  local copies, waits for them, and re-layouts: 98.7 us -> 37.5 us
  starting transfers between devices: 62.8 us -> 122 us
  blocking collectives: 0 us -> 46.3 us
  between operations: 16.6 us -> 0.96 us
    pallas_call x0 -> x8, Pallas kernels: none -> 459 us  [the longest x2 400 us: attend_last(): pl.pallas_call(functools.partial(last_kernel, span, groups, first_row, 10...]
    dot_general x51 -> x3, matrix products: 214 us -> 11.1 us  [the longest x2 9.93 us: project(): part = jnp.dot(attended, w_out, preferred_element_type=F32).astype(BF16)]
    all_to_all x7 -> x3, waiting for transfers between devices: 101 us -> 19.7 us  [exchange(): return lax.all_to_all(block, axis, split_axis=0, concat_axis=0, tiled=True)]
    reduce_sum x27 -> x4, other arithmetic: 72.3 us -> 0.66 us  [the longest x1 0.23 us: shards(): rank = jnp.sum((same & earlier).astype(jnp.int32), axis=-1)]
    all_to_all x7 -> x3, starting transfers between devices: 46.9 us -> 103 us  [exchange(): return lax.all_to_all(block, axis, split_axis=0, concat_axis=0, tiled=True)]
    reduce_scatter x3 -> x0, waiting for transfers between devices: 52.1 us -> none  [shards(): lax.psum_scatter(jnp.dot(attended, w_out, preferred_element_type=jnp.floa...]
    all_to_all x0 -> x1, blocking collectives: none -> 46.3 us  [exchange(): return lax.all_to_all(block, axis, split_axis=0, concat_axis=0, tiled=True)]
    reshape x7 -> x1, local copies, waits for them, and re-layouts: 22.8 us -> 0.07 us  [shards(): ids = expert_ids.reshape(steps, assigned)]
  transfers between devices with their start and end apart: 22 -> 17, of which waited for: 9 -> 8; matrix products, arithmetic and copies ran while one was open for 43% -> 7% of each run, Pallas kernels for 0% -> 59%
where the time goes in v1:
time: 742 us; the launch traced here: 733 us
  Pallas kernels  459 us (62%)
  starting transfers between devices  122 us (16%)
  blocking collectives  46.3 us (6%)
  waiting for transfers between devices  40.4 us (5%)
  local copies, waits for them, and re-layouts  37.5 us (5%)
  other arithmetic  16 us (2%)
  matrix products  11.1 us (1%)
    pallas_call x2, Pallas kernels, attend_last(): pl.pallas_call(functools.partial(last_kernel, span, groups, first_row, 10...  400 us
    all_to_all x3, starting transfers between devices, exchange(): return lax.all_to_all(block, axis, split_axis=0, concat_axis=0, tiled=True)  103 us
    all_to_all x1, blocking collectives, exchange(): return lax.all_to_all(block, axis, split_axis=0, concat_axis=0, tiled=True)  46.3 us
    pallas_call x2, Pallas kernels, attend_first(): pl.pallas_call(functools.partial(first_kernel, span, groups, 1024, 2048),...  30.6 us
    unnamed x43, local copies, waits for them, and re-layouts  22 us
    pallas_call x1, Pallas kernels, expert_rows(): pl.pallas_call(expert_kernel, out_shape=(jax.ShapeDtypeStruct(own.shape,...  20.1 us
    all_to_all x3, waiting for transfers between devices, exchange(): return lax.all_to_all(block, axis, split_axis=0, concat_axis=0, tiled=True)  19.7 us
  transfers between devices with their start and end apart: 17, of which 8 were waited for; matrix products, arithmetic and copies ran while one was open for 7% of the time, Pallas kernels for 59%

profile of v1, /device:TPU:0, one launch (start us, length us, event | category | flops | bytes accessed | tf_op | source)
XLA Modules:
  0.0 733.2 jit_solution(14525751932977786769)
XLA Ops:
  2.2 5.0 split_heads.1
  8.5 7.1 all-to-all-start
  19.6 4.0 collective-permute-start.10
  23.8 11.8 %copy.62 = bf16[1,2880,2,720]{3,1,2,0:T(8,128)(2,1)} copy(bf16[1,2880,2,720]{1,3,2,0:T(8,128)(2,1)} %param.22) | data formatting | bytes 16588800 | tf_op args[10]
  37.8 9.5 %all-to-all-done = bf16[16,512,128]{2,1,0:T(8,128)(2,1)S(1)} async-done(((bf16[16,512,128]{2,1,0:T(8,128)(2,1)}), bf16[16,512,128]{2,1,0:T(8,128)(2,1)S(1)}, u32[]{:S(2)}, u32[]{:S(2)}) %all-to-all-start) | async-done | bytes 2097184 | tf_op jit(solution)/shard_map/all_to_all | solution.py:47
  47.3 4.4 all-to-all-start.1
  51.7 20.5 %attend_first.2.acc_in_ref = f32[2048,128]{1,0:T(8,128)S(1)} custom-call(s32[2]{0:T(128)S(1)} %pad_add_fusion.at_ref, bf16[256,512]{1,0:T(8,128)(2,1)S(1)} %bitcast.117, bf16[8192,128]{1,0:T(8,128)(2,1)S(1)} %bitcast.108), custom_call_target="tpu_custom_call" | custom-call | flops 17179869184 | bytes 2097152 | tf_op jit(solution)/shard_map/attend_first/pallas_call | solution.py:227
  73.2 10.1 %attend_first.3.acc_in_ref = f32[1024,128]{1,0:T(8,128)S(1)} custom-call(s32[2]{0:T(128)S(1)} %pad_add_fusion.at_ref, bf16[128,512]{1,0:T(8,128)(2,1)S(1)} %fusion.8.q_ref, bf16[8192,128]{1,0:T(8,128)(2,1)S(1)} %bitcast.109), custom_call_target="tpu_custom_call" | custom-call | flops 8589934592 | bytes 2097152 | tf_op jit(solution)/shard_map/attend_first/pallas_call | solution.py:227
  85.4 264.5 %attend_last.2 = bf16[256,512]{1,0:T(8,128)(2,1)S(1)} custom-call(s32[2]{0:T(128)S(1)} %pad_add_fusion.at_ref, f32[8]{0:T(128)S(1)} %dynamic_slice.33.sink_ref, bf16[256,512]{1,0:T(8,128)(2,1)S(1)} %bitcast.118, bf16[384,128]{1,0:T(8,128)(2,1)S(1)} %bitcast.120, bf16[8192,128]{1,0:T(8,128)(2,1)S(1)} %bitcast.110, bf16[8192,128]{1,0:T(8,128)(2,1)} %bitcast.12.kv_far_ref, ...), custom_call_target="tpu_custom_call" | custom-call | flops 17179869184 | bytes 2097152 | tf_op jit(solution)/shard_map/attend_last/pallas_call | solution.py:242
  351.4 5.3 convolution_convert_fusion
  359.0 135.6 %attend_last.3 = bf16[128,512]{1,0:T(8,128)(2,1)S(1)} custom-call(s32[2]{0:T(128)S(1)} %pad_add_fusion.at_ref, f32[8]{0:T(128)S(1)} %dynamic_slice.33.sink_ref, bf16[128,512]{1,0:T(8,128)(2,1)S(1)} %fusion.8.q_ref, bf16[384,128]{1,0:T(8,128)(2,1)S(1)} %bitcast.121, bf16[8192,128]{1,0:T(8,128)(2,1)S(1)} %bitcast.111, bf16[8192,128]{1,0:T(8,128)(2,1)} %bitcast.12.kv_far_ref, ...), custom_call_target="tpu_custom_call" | custom-call | flops 8589934592 | bytes 2097152 | tf_op jit(solution)/shard_map/attend_last/pallas_call | solution.py:242
  497.2 3.6 collective-permute-start.4
  501.8 4.6 convolution_convert_fusion.1
  506.4 3.3 collective-permute-done.4
  514.5 5.2 collective-permute-done.9
  523.6 91.5 %all-to-all-start.2 = ((bf16[64,8,2944]{2,1,0:T(8,128)(2,1)}), bf16[64,8,2944]{2,1,0:T(8,128)(2,1)S(1)}, u32[]{:S(2)}, u32[]{:S(2)}) async-start(bf16[64,8,2944]{2,1,0:T(8,128)(2,1)} %bitcast.37), calls=%async_computation.2 | async-start | bytes 6029312 | tf_op jit(solution)/shard_map/all_to_all | solution.py:47
  616.6 11.9 %copy.70 = bf16[1,2880,2,720]{3,1,2,0:T(8,128)(2,1)} copy(bf16[1,2880,2,720]{1,3,2,0:T(8,128)(2,1)} %collective-permute-done.10) | data formatting | bytes 16588800 | tf_op jit(solution)/shard_map/optimization_barrier | solution.py:39
  628.8 5.0 select_bitcast_fusion.down_ref
  635.1 7.5 %bitcast_select_fusion.gate_up_ref = bf16[2,2880,720]{2,1,0:T(8,128)(2,1)} fusion(bf16[2,2880,720]{2,1,0:T(8,128)(2,1)} %bitcast.122, bf16[1,2880,2,720]{3,1,2,0:T(8,128)(2,1)S(1)} %copy-done.8, pred[]{:T(512)S(6)} %ne.75), kind=kLoop, calls=%fused_computation | loop fusion | flops 4147200 | bytes 24883200 | tf_op jit(solution)/shard_map/jit(_where)/select_n | solution.py:525
  642.6 10.2 %all-to-all-done.2 = bf16[64,8,2944]{2,1,0:T(8,128)(2,1)S(1)} async-done(((bf16[64,8,2944]{2,1,0:T(8,128)(2,1)}), bf16[64,8,2944]{2,1,0:T(8,128)(2,1)S(1)}, u32[]{:S(2)}, u32[]{:S(2)}) %all-to-all-start.2) | async-done | bytes 3014688 | tf_op jit(solution)/shard_map/all_to_all | solution.py:47
  653.1 5.5 collective-permute-done.12.other_ref
  658.5 20.1 %expert_rows.1 = (bf16[512,2944]{1,0:T(8,128)(2,1)S(1)}, bf16[512,2944]{1,0:T(8,128)(2,1)S(1)}) custom-call(bf16[512,2944]{1,0:T(8,128)(2,1)S(1)} %bitcast.107, bf16[512,2944]{1,0:T(8,128)(2,1)S(1)} %collective-permute-done.12.other_ref, bf16[2,2880,720]{2,1,0:T(8,128)(2,1)} %bitcast_select_fusion.gate_up_ref, bf16[720,2880]{1,0:T(8,128)(2,1)} %select_bitcast_fusion.down_ref), custom_call_target="tpu_custom_call" | custom-call | flops 12740198400 | bytes 24500224 | tf_op jit(solution)/shard_map/expert_rows/pallas_call | solution.py:340
  678.9 5.3 collective-permute-done.13
  685.0 46.3 %all_to_all.20 = bf16[64,8,2944]{2,1,0:T(8,128)(2,1)S(1)} all-to-all(bf16[64,8,2944]{2,1,0:T(8,128)(2,1)S(1)} %fusion), channel_id=1, replica_groups=mesh['chip'=16,'core'=2,'z'=4] {'chip','z'}, dimensions={0} | all-to-all | bytes 6029312 | tf_op jit(solution)/shard_map/all_to_all | solution.py:47
  (111 shorter events, 34.3 us)
Async XLA Ops:
  0.0 615.1 %copy-start = (bf16[2880,64]{0,1:T(8,128)(2,1)S(1)}, bf16[2880,64]{0,1:T(8,128)(2,1)}, u32[]{:S(2)}) copy-start(bf16[2880,64]{0,1:T(8,128)(2,1)} %param.20) | copy-start | bytes 1105924
  2.2 14.4 %copy-start.15 = (bf16[3,64,2,128]{3,2,1,0:T(2,128)(2,1)S(1)}, bf16[3,64,2,128]{3,2,1,0:T(2,128)(2,1)}, u32[]{:S(2)}) copy-start(bf16[3,64,2,128]{3,2,1,0:T(2,128)(2,1)} %param.15) | copy-start | bytes 294916
  7.2 40.1 %collective-permute-start.1 = (bf16[16,512,128]{2,1,0:T(8,128)(2,1)}, bf16[16,512,128]{2,1,0:T(8,128)(2,1)}, u32[]{:S(2)}, u32[]{:S(2)}) collective-permute-start(bf16[16,512,128]{2,1,0:T(8,128)(2,1)} %bitcast.11), channel_id=1, source_target_pairs={{0,4},{4,0},{1,5},{5,1},{2,6},{6,2},{3,7},{7,3},{8,12},{12,8},{9,1... | collective-permute-start | bytes 6291464 | tf_op jit(solution)/shard_map/ppermute | solution.py:22
  8.5 38.8 %all-to-all-start = ((bf16[16,512,128]{2,1,0:T(8,128)(2,1)}), bf16[16,512,128]{2,1,0:T(8,128)(2,1)S(1)}, u32[]{:S(2)}, u32[]{:S(2)}) async-start(bf16[16,512,128]{2,1,0:T(8,128)(2,1)} %bitcast.112), calls=%async_computation | async-start | bytes 4194304 | tf_op jit(solution)/shard_map/all_to_all | solution.py:47
  16.8 20.9 %collective-permute-start = (bf16[3,64,640]{2,1,0:T(8,128)(2,1)S(1)}, bf16[3,64,640]{2,1,0:T(8,128)(2,1)S(1)}, u32[]{:S(2)}, u32[]{:S(2)}) collective-permute-start(bf16[3,64,640]{2,1,0:T(8,128)(2,1)S(1)} %select_bitcast_fusion.1), channel_id=1, source_target_pairs={{0,4},{4,0},{1,5},{5,1},{2,6},{6,2},{3,7},{7,3},{8,12},{12,8},{9,1... | collective-permute-start | bytes 737288 | tf_op jit(solution)/shard_map/ppermute | solution.py:22
  16.9 506.8 %collective-permute-start.11 = (bf16[1,720,2880]{2,1,0:T(8,128)(2,1)}, bf16[1,720,2880]{2,1,0:T(8,128)(2,1)}, u32[]{:S(2)}, u32[]{:S(2)}) collective-permute-start(bf16[1,720,2880]{2,1,0:T(8,128)(2,1)} %param.23), channel_id=1, source_target_pairs={{4,1},{1,4},{6,3},{3,6},{12,9},{9,12},{14,11},{11,14},{20,17},{17,... | collective-permute-start | bytes 12441608 | tf_op jit(solution)/shard_map/ppermute | solution.py:35
  19.6 504.0 %collective-permute-start.10 = (bf16[1,2880,2,720]{1,3,2,0:T(8,128)(2,1)}, bf16[1,2880,2,720]{1,3,2,0:T(8,128)(2,1)}, u32[]{:S(2)}, u32[]{:S(2)}) collective-permute-start(bf16[1,2880,2,720]{1,3,2,0:T(8,128)(2,1)} %param.22), channel_id=1, source_target_pairs={{4,1},{1,4},{6,3},{3,6},{12,9},{9,12},{14,11},{11,14},{20,17},{17,... | collective-permute-start | bytes 24883208 | tf_op jit(solution)/shard_map/ppermute | solution.py:35
  47.3 36.9 %all-to-all-start.1 = ((bf16[16,512,128]{2,1,0:T(8,128)(2,1)}), bf16[16,512,128]{2,1,0:T(8,128)(2,1)}, u32[]{:S(2)}, u32[]{:S(2)}) async-start(bf16[16,512,128]{2,1,0:T(8,128)(2,1)} %collective-permute-done.1), calls=%async_computation.1 | async-start | bytes 4194304 | tf_op jit(solution)/shard_map/all_to_all | solution.py:47
  349.9 1.4 collective-permute-start.2
  359.0 136.1 %copy-start.11 = (bf16[128,2880]{1,0:T(8,128)(2,1)S(1)}, bf16[128,2880]{1,0:T(8,128)(2,1)}, u32[]{:S(2)}) copy-start(bf16[128,2880]{1,0:T(8,128)(2,1)} %copy.66) | copy-start | bytes 2211844
  494.7 19.5 %slice-start = ((bf16[3,16,2880]{2,1,0:T(8,128)(2,1)}), bf16[2,16,2880]{2,1,0:T(8,128)(2,1)S(1)}, s32[]{:S(2)}) async-start(bf16[3,16,2880]{2,1,0:T(8,128)(2,1)} %param.17), calls=%async_computation.4 | async-start | bytes 376832 | tf_op jit(solution)/shard_map/slice | solution.py:454
  494.7 6.1 collective-permute-start.6
  495.2 11.2 %collective-permute-start.5 = (bf16[32,2880]{1,0:T(8,128)(2,1)S(1)}, bf16[32,2880]{1,0:T(8,128)(2,1)S(1)}, u32[]{:S(2)}, u32[]{:S(2)}) collective-permute-start(bf16[32,2880]{1,0:T(8,128)(2,1)S(1)} %get-tuple-element.55), channel_id=1, source_target_pairs={{0,1},{1,2},{2,3},{3,0},{4,5},{5,6},{6,7},{7,4},{8,9},{9,10},{10,1... | collective-permute-start | bytes 552968 | tf_op jit(solution)/shard_map/ppermute | solution.py:27
  497.2 12.6 %collective-permute-start.4 = (bf16[32,2880]{1,0:T(8,128)(2,1)S(1)}, bf16[32,2880]{1,0:T(8,128)(2,1)S(1)}, u32[]{:S(2)}, u32[]{:S(2)}) collective-permute-start(bf16[32,2880]{1,0:T(8,128)(2,1)S(1)} %get-tuple-element.56), channel_id=1, source_target_pairs={{0,2},{1,3},{2,0},{3,1},{4,6},{5,7},{6,4},{7,5},{8,10},{9,11},{10,... | collective-permute-start | bytes 552968 | tf_op jit(solution)/shard_map/ppermute | solution.py:27
  500.8 18.8 %copy-start.14 = (bf16[3,16,2880]{2,1,0:T(8,128)(2,1)S(1)}, bf16[3,16,2880]{2,1,0:T(8,128)(2,1)}, u32[]{:S(2)}) copy-start(bf16[3,16,2880]{2,1,0:T(8,128)(2,1)} %param.17) | copy-start | bytes 829444
  500.8 9.0 %collective-permute-start.3 = (bf16[32,2880]{1,0:T(8,128)(2,1)S(1)}, bf16[32,2880]{1,0:T(8,128)(2,1)S(1)}, u32[]{:S(2)}, u32[]{:S(2)}) collective-permute-start(bf16[32,2880]{1,0:T(8,128)(2,1)S(1)} %get-tuple-element.57), channel_id=1, source_target_pairs={{0,3},{1,0},{2,1},{3,2},{4,7},{5,4},{6,5},{7,6},{8,11},{9,8},{10,9... | collective-permute-start | bytes 552968 | tf_op jit(solution)/shard_map/ppermute | solution.py:27
  509.8 4.6 collective-permute-start.7
  512.0 7.6 %collective-permute-start.9 = (bf16[16,2880]{1,0:T(8,128)(2,1)S(1)}, bf16[16,2880]{1,0:T(8,128)(2,1)S(1)}, u32[]{:S(2)}, u32[]{:S(2)}) collective-permute-start(bf16[16,2880]{1,0:T(8,128)(2,1)S(1)} %get-tuple-element.64), channel_id=1, source_target_pairs={{0,1},{1,2},{2,3},{3,0},{4,5},{5,6},{6,7},{7,4},{8,9},{9,10},{10,1... | collective-permute-start | bytes 276488 | tf_op jit(solution)/shard_map/ppermute | solution.py:27
  512.0 7.6 %collective-permute-start.8 = (bf16[16,2880]{1,0:T(8,128)(2,1)S(1)}, bf16[16,2880]{1,0:T(8,128)(2,1)S(1)}, u32[]{:S(2)}, u32[]{:S(2)}) collective-permute-start(bf16[16,2880]{1,0:T(8,128)(2,1)S(1)} %get-tuple-element.65), channel_id=1, source_target_pairs={{0,2},{1,3},{2,0},{3,1},{4,6},{5,7},{6,4},{7,5},{8,10},{9,11},{10,... | collective-permute-start | bytes 276488 | tf_op jit(solution)/shard_map/ppermute | solution.py:27
  523.6 129.2 %all-to-all-start.2 = ((bf16[64,8,2944]{2,1,0:T(8,128)(2,1)}), bf16[64,8,2944]{2,1,0:T(8,128)(2,1)S(1)}, u32[]{:S(2)}, u32[]{:S(2)}) async-start(bf16[64,8,2944]{2,1,0:T(8,128)(2,1)} %bitcast.37), calls=%async_computation.2 | async-start | bytes 6029312 | tf_op jit(solution)/shard_map/all_to_all | solution.py:47
  652.8 5.7 collective-permute-start.12
  678.7 5.6 collective-permute-start.13
  684.9 47.1 %copy-start.10 = (f32[32,2880]{1,0:T(8,128)S(1)}, f32[32,2880]{1,0:T(8,128)}, u32[]{:S(2)}) copy-start(f32[32,2880]{1,0:T(8,128)} %copy-done.9) | copy-start | bytes 1105924
  685.0 47.1 %copy-start.13 = (f32[16,2880]{1,0:T(8,128)S(1)}, f32[16,2880]{1,0:T(8,128)}, u32[]{:S(2)}) copy-start(f32[16,2880]{1,0:T(8,128)} %copy-done.12) | copy-start | bytes 552964
  (14 other events, 76.8 us)

commit v2 on v1

--- a/solution.py
+++ b/solution.py
@@ -55,17 +55,16 @@
     return (length // (2 * span)) * span + jnp.clip(length % (2 * span) - core * span, 0, span)
 
 
-def fill_queries(q_ref, qs_ref, rows, groups):
-    lane = lane_ids((rows, LANES))
-    extra = jnp.where(lane == HEAD, 1.0, 0.0)
+def fill_queries(q_ref, qt_ref, rows, groups):
+    row = lax.broadcasted_iota(jnp.int32, (HEAD, rows), 0)
+    extra = jnp.where(row == 0, 1.0, 0.0).astype(BF16)
     for pair in range(groups // 2):
         both = q_ref[:, pair * LANES : (pair + 1) * LANES].astype(F32) * 0.125
+        turned = both.T.astype(BF16)
         for side in range(2):
-            group = 2 * pair + side
-            part = both if side == 0 else pltpu.roll(both, HEAD, 1)
-            qs_ref[group * rows : (group + 1) * rows, :] = jnp.where(
-                lane < HEAD, part, extra
-            ).astype(BF16)
+            first = (2 * pair + side) * rows
+            qt_ref[:HEAD, first : first + rows] = turned[side * HEAD : (side + 1) * HEAD]
+            qt_ref[HEAD:, first : first + rows] = extra
 
 
 def key_value_rows(block, first, valid):
@@ -75,22 +74,22 @@
     bias = jnp.where(position < valid, 0.0, NEG).astype(BF16)
     keys = jnp.where(lane == HEAD, bias, block)
     values = jnp.where(lane < HEAD, jnp.ones_like(block), block)
-    return keys, values
-
-
-def score(query_rows, keys):
-    return lax.dot_general(query_rows, keys, (((1,), (1,)), ((), ())), preferred_element_type=F32)
-
-
-def add_chunk(qs_ref, kv_ref, acc_ref, valid, total_rows, query_span, key_span):
+    return keys, values.T
+
+
+def score(keys, turned_queries):
+    return jnp.dot(keys, turned_queries, preferred_element_type=F32)
+
+
+def add_chunk(qt_ref, kv_ref, acc_ref, valid, total_rows, query_span, key_span):
     def key_block(index, carry):
         first = pl.multiple_of(index * key_span, key_span)
         keys, values = key_value_rows(kv_ref[pl.ds(first, key_span), :], first, valid)
 
         def query_block(number, inner):
             at = pl.ds(pl.multiple_of(number * query_span, query_span), query_span)
-            weights = jnp.exp(score(qs_ref[at, :], keys)).astype(BF16)
-            acc_ref[at, :] += jnp.dot(weights, values, preferred_element_type=F32)
+            weights = jnp.exp(score(keys, qt_ref[:, at])).astype(BF16)
+            acc_ref[:, at] += jnp.dot(values, weights, preferred_element_type=F32)
             return inner
 
         return lax.fori_loop(0, total_rows // query_span, query_block, carry)
@@ -99,21 +98,21 @@
 
 
 def safe_update(scores, values, at, acc_ref, peak_ref):
-    old = peak_ref[at, :]
-    new = jnp.maximum(old, jnp.max(scores, axis=1, keepdims=True))
-    weights = jnp.exp(scores - new[:, :1]).astype(BF16)
-    acc_ref[at, :] = acc_ref[at, :] * jnp.exp(old - new) + jnp.dot(
-        weights, values, preferred_element_type=F32
-    )
-    peak_ref[at, :] = new
-
-
-def first_kernel(span, groups, query_span, key_span, at_ref, q_ref, kv_ref, acc_ref, qs_ref):
+    old = peak_ref[0:1, at]
+    new = jnp.maximum(old, jnp.max(scores, axis=0, keepdims=True))
+    weights = jnp.exp(scores - new).astype(BF16)
+    acc_ref[:, at] = acc_ref[:, at] * jnp.exp(old - new) + jnp.dot(
+        values, weights, preferred_element_type=F32
+    )
+    peak_ref[:, at] = jnp.broadcast_to(new, (peak_ref.shape[0], new.shape[1]))
+
+
+def first_kernel(span, groups, query_span, key_span, at_ref, q_ref, kv_ref, acc_ref, qt_ref):
     rows = q_ref.shape[0]
-    fill_queries(q_ref, qs_ref, rows, groups)
+    fill_queries(q_ref, qt_ref, rows, groups)
     acc_ref[...] = jnp.zeros_like(acc_ref)
     valid = valid_rows(at_ref[0], span, at_ref[1])
-    add_chunk(qs_ref, kv_ref, acc_ref, valid, rows * groups, query_span, key_span)
+    add_chunk(qt_ref, kv_ref, acc_ref, valid, rows * groups, query_span, key_span)
 
 
 def last_kernel(
@@ -131,30 +130,29 @@
     acc_in_ref,
     out_ref,
     acc_ref,
-    qs_ref,
+    qt_ref,
     peak_ref,
 ):
     rows = q_ref.shape[0]
     recents = recent_ref.shape[0]
     total = rows * groups
-    fill_queries(q_ref, qs_ref, rows, groups)
+    fill_queries(q_ref, qt_ref, rows, groups)
     recent_keys, recent_values = key_value_rows(recent_ref[...], 0, recents)
-    row_id = lax.broadcasted_iota(jnp.int32, (rows, recents), 0) + first_row
-    causal = lane_ids((rows, recents)) <= row_id
+    key_id = lax.broadcasted_iota(jnp.int32, (recents, rows), 0)
+    causal = key_id <= lane_ids((recents, rows)) + first_row
 
     def recent_scores(group):
-        at = pl.ds(group * rows, rows)
-        return jnp.where(causal, score(qs_ref[at, :], recent_keys), NEG)
+        return jnp.where(causal, score(recent_keys, qt_ref[:, pl.ds(group * rows, rows)]), NEG)
 
     for group in range(groups):
         at = pl.ds(group * rows, rows)
         weights = jnp.exp(recent_scores(group)).astype(BF16)
-        gained = jnp.dot(weights, recent_values, preferred_element_type=F32)
-        acc_ref[at, :] = acc_in_ref[at, :] + gained
+        acc_ref[:, at] = acc_in_ref[:, at] + jnp.dot(
+            recent_values, weights, preferred_element_type=F32
+        )
     near = valid_rows(at_ref[0], span, at_ref[1])
     far = valid_rows(at_ref[0], span, 1 - at_ref[1])
-    add_chunk(qs_ref, kv_far_ref, acc_ref, far, total, query_span, key_span)
-    lane = lane_ids((rows, LANES))
+    add_chunk(qt_ref, kv_far_ref, acc_ref, far, total, query_span, key_span)
 
     def finish(shifted):
         for pair in range(groups // 2):
@@ -162,20 +160,14 @@
             for side in range(2):
                 group = 2 * pair + side
                 at = pl.ds(group * rows, rows)
-                sink = jnp.full((rows, LANES), sink_ref[group], F32)
-                own = jnp.exp(sink - peak_ref[at, :]) if shifted else jnp.exp(sink)
-                value = acc_ref[at, :]
-                if side == 0:
-                    halves.append(pltpu.roll(value, HEAD, 1) / (value + own))
-                else:
-                    halves.append(value / (pltpu.roll(value, HEAD, 1) + own))
-            out_ref[:, pair * LANES : (pair + 1) * LANES] = jnp.where(
-                lane < HEAD, halves[0], halves[1]
-            ).astype(BF16)
-
-    acc_lane = lane_ids((total, LANES))
-    weight_sums = jnp.where(acc_lane < HEAD, acc_ref[...], 0.0)
-    fits = jnp.max(jnp.where(weight_sums < LIMIT, 0.0, 1.0)) == 0.0
+                sink = jnp.full((HEAD, rows), sink_ref[group], F32)
+                own = jnp.exp(sink - peak_ref[0:1, at]) if shifted else jnp.exp(sink)
+                halves.append(acc_ref[HEAD:, at] / (acc_ref[:HEAD, at] + own))
+            out_ref[:, pair * LANES : (pair + 1) * LANES] = (
+                jnp.concatenate(halves, axis=0).T.astype(BF16)
+            )
+
+    fits = jnp.max(jnp.where(acc_ref[:HEAD, :] < LIMIT, 0.0, 1.0)) == 0.0
 
     @pl.when(fits)
     def plain():
@@ -186,7 +178,7 @@
         acc_ref[...] = jnp.zeros_like(acc_ref)
         for group in range(groups):
             at = pl.ds(group * rows, rows)
-            peak_ref[at, :] = jnp.full((rows, LANES), sink_ref[group], F32)
+            peak_ref[:, at] = jnp.full((peak_ref.shape[0], rows), sink_ref[group], F32)
             safe_update(recent_scores(group), recent_values, at, acc_ref, peak_ref)
         block = 256
         for kv_ref, limit in ((kv_near_ref, near), (kv_far_ref, far)):
@@ -197,7 +189,7 @@
 
                 def query_block(number, inner):
                     at = pl.ds(pl.multiple_of(number * block, block), block)
-                    safe_update(score(qs_ref[at, :], keys), values, at, acc_ref, peak_ref)
+                    safe_update(score(keys, qt_ref[:, at]), values, at, acc_ref, peak_ref)
                     return inner
 
                 return lax.fori_loop(0, total // block, query_block, carry)
@@ -226,10 +218,10 @@
     total = rows * groups
     return pl.pallas_call(
         functools.partial(first_kernel, span, groups, 1024, 2048),
-        out_shape=jax.ShapeDtypeStruct((total, LANES), F32),
+        out_shape=jax.ShapeDtypeStruct((LANES, total), F32),
         in_specs=[SMEM_SPEC, VMEM_SPEC, VMEM_SPEC],
         out_specs=VMEM_SPEC,
-        scratch_shapes=[pltpu.VMEM((total, LANES), BF16)],
+        scratch_shapes=[pltpu.VMEM((LANES, total), BF16)],
         compiler_params=ATTEND,
         cost_estimate=attention_cost(rows, groups, kv.shape[0]),
         name="attend_first",
@@ -245,9 +237,9 @@
         in_specs=[SMEM_SPEC, SMEM_SPEC] + [VMEM_SPEC] * 5,
         out_specs=VMEM_SPEC,
         scratch_shapes=[
-            pltpu.VMEM((total, LANES), F32),
-            pltpu.VMEM((total, LANES), BF16),
-            pltpu.VMEM((total, LANES), F32),
+            pltpu.VMEM((LANES, total), F32),
+            pltpu.VMEM((LANES, total), BF16),
+            pltpu.VMEM((8, total), F32),
         ],
         compiler_params=ATTEND,
         cost_estimate=attention_cost(rows, groups, far.shape[0]),
@@ -316,7 +308,7 @@
 
 
 def expert_kernel(own_ref, other_ref, gate_up_ref, down_ref, own_out_ref, other_out_ref):
-    tile = 256
+    tile = own_ref.shape[0]
     width = down_ref.shape[1]
     for rows_ref, out_ref in ((own_ref, own_out_ref), (other_ref, other_out_ref)):
 
@@ -441,7 +433,7 @@
     earlier = jnp.arange(assigned)[:, None] > jnp.arange(assigned)[None, :]
     same = ids[..., :, None] == ids[..., None, :]
     rank = jnp.sum((same & earlier).astype(jnp.int32), axis=-1)
-    stride = round_up(steps * capacity, 8)
+    stride = steps * capacity
     kind = ids % 4
     target = (ids // 4) * depth + 2 * (kind % 2) + kind // 2
     step_ids = jnp.arange(steps, dtype=jnp.int32)[:, None]
@@ -520,7 +512,7 @@
     rows = normalize(hidden)
     sent = pack_rows(jnp.transpose(slot), rows, slots)
     sent, far_gate_up, far_down, rows = tie(sent, far_gate_up, far_down, rows)
-    arrived = exchange(sent.reshape(experts, stride, padded), ("chip", "z"))
+    arrived = exchange(sent.reshape(experts * steps, capacity, padded), ("chip", "z"))
     far_gate_up = jnp.transpose(far_gate_up[0], (1, 0, 2))
     gate_up = jnp.where(swapped, far_gate_up, near_gate_up)
     down = jnp.where(swapped, far_down, w_down)[0]
@@ -529,7 +521,7 @@
     arrived = arrived.reshape(slots, padded)
     own, other = expert_rows(arrived, partner(arrived), gate_up, down)
     done = (own.astype(F32) + partner(other).astype(F32)).astype(BF16)
-    returned = exchange(done.reshape(experts, stride, padded), ("chip", "z"))
+    returned = exchange(done.reshape(experts * steps, capacity, padded), ("chip", "z"))
     mixed = blend_rows(slot, gates, returned.reshape(slots, padded))
     out = (hidden + mixed[:, :model_dim]).astype(BF16)
     return out.reshape(steps, rows_dev, model_dim)

time: 742 us -> 602 us (0.81)
  starting transfers between devices: 122 us -> 35.7 us
  Pallas kernels: 459 us -> 410 us
  local copies, waits for them, and re-layouts: 37.5 us -> 50.6 us
  blocking collectives: 46.3 us -> 38.1 us
    all_to_all x3, starting transfers between devices: 103 us -> 17.3 us  [exchange(): return lax.all_to_all(block, axis, split_axis=0, concat_axis=0, tiled=True)]
    pallas_call x2, Pallas kernels: 400 us -> 365 us  [attend_last(): pl.pallas_call(functools.partial(last_kernel, span, groups, first_row, 10...]
    reshape x0 -> x4, local copies, waits for them, and re-layouts: none -> 10.3 us  [the longest x1 2.82 us: shards(): arrived = arrived.reshape(slots, padded)]
    all_to_all x1, blocking collectives: 46.3 us -> 38.1 us  [exchange(): return lax.all_to_all(block, axis, split_axis=0, concat_axis=0, tiled=True)]
    unnamed x43 -> x33, local copies, waits for them, and re-layouts: 22 us -> 24.2 us
  transfers between devices with their start and end apart: 17 -> 17, of which waited for: 8 -> 9; matrix products, arithmetic and copies ran while one was open for 7% -> 9% of each run, Pallas kernels for 59% -> 65%
where the time goes in v2:
time: 602 us; the launch traced here: 597 us
  Pallas kernels  410 us (68%)
  local copies, waits for them, and re-layouts  50.6 us (8%)
  blocking collectives  38.1 us (6%)
  starting transfers between devices  35.7 us (6%)
  waiting for transfers between devices  35.3 us (6%)
  other arithmetic  15.9 us (3%)
  matrix products  10.1 us (2%)
    pallas_call x2, Pallas kernels, attend_last(): pl.pallas_call(functools.partial(last_kernel, span, groups, first_row, 10...  365 us
    all_to_all x1, blocking collectives, exchange(): return lax.all_to_all(block, axis, split_axis=0, concat_axis=0, tiled=True)  38.1 us
    unnamed x33, local copies, waits for them, and re-layouts  24.2 us
    pallas_call x2, Pallas kernels, attend_first(): pl.pallas_call(functools.partial(first_kernel, span, groups, 1024, 2048),...  24.1 us
    all_to_all x3, starting transfers between devices, exchange(): return lax.all_to_all(block, axis, split_axis=0, concat_axis=0, tiled=True)  17.3 us
    all_to_all x3, waiting for transfers between devices, exchange(): return lax.all_to_all(block, axis, split_axis=0, concat_axis=0, tiled=True)  16.7 us
    pallas_call x1, Pallas kernels, expert_rows(): pl.pallas_call(expert_kernel, out_shape=(jax.ShapeDtypeStruct(own.shape,...  14.8 us
  transfers between devices with their start and end apart: 17, of which 9 were waited for; matrix products, arithmetic and copies ran while one was open for 9% of the time, Pallas kernels for 65%

profile of v2, /device:TPU:0, one launch (start us, length us, event | category | flops | bytes accessed | tf_op | source)
XLA Modules:
  0.0 596.8 jit_solution(10530143784321779494)
XLA Ops:
  2.2 5.0 split_heads.1
  8.5 7.1 %all-to-all-start = ((bf16[16,512,128]{2,1,0:T(8,128)(2,1)}), bf16[16,512,128]{2,1,0:T(8,128)(2,1)S(1)}, u32[]{:S(2)}, u32[]{:S(2)}) async-start(bf16[16,512,128]{2,1,0:T(8,128)(2,1)} %bitcast.104), calls=%async_computation | async-start | bytes 4194304 | tf_op jit(solution)/shard_map/all_to_all | solution.py:47
  19.6 4.0 collective-permute-start.10
  23.8 11.9 %copy.62 = bf16[1,2880,2,720]{3,1,2,0:T(8,128)(2,1)} copy(bf16[1,2880,2,720]{1,3,2,0:T(8,128)(2,1)} %param.22) | data formatting | bytes 16588800 | tf_op args[10]
  38.6 8.7 %all-to-all-done = bf16[16,512,128]{2,1,0:T(8,128)(2,1)S(1)} async-done(((bf16[16,512,128]{2,1,0:T(8,128)(2,1)}), bf16[16,512,128]{2,1,0:T(8,128)(2,1)S(1)}, u32[]{:S(2)}, u32[]{:S(2)}) %all-to-all-start) | async-done | bytes 2097184 | tf_op jit(solution)/shard_map/all_to_all | solution.py:47
  47.3 4.4 all-to-all-start.1
  51.8 16.0 %attend_first.2.acc_in_ref = f32[128,2048]{1,0:T(8,128)S(1)} custom-call(s32[2]{0:T(128)S(1)} %pad_add_fusion.at_ref, bf16[256,512]{1,0:T(8,128)(2,1)S(1)} %bitcast.109, bf16[8192,128]{1,0:T(8,128)(2,1)S(1)} %bitcast.100), custom_call_target="tpu_custom_call" | custom-call | flops 17179869184 | bytes 2097152 | tf_op jit(solution)/shard_map/attend_first/pallas_call | solution.py:219
  68.8 8.0 %attend_first.3.acc_in_ref = f32[128,1024]{1,0:T(8,128)S(1)} custom-call(s32[2]{0:T(128)S(1)} %pad_add_fusion.at_ref, bf16[128,512]{1,0:T(8,128)(2,1)S(1)} %fusion.7.q_ref, bf16[8192,128]{1,0:T(8,128)(2,1)S(1)} %bitcast.101), custom_call_target="tpu_custom_call" | custom-call | flops 8589934592 | bytes 2097152 | tf_op jit(solution)/shard_map/attend_first/pallas_call | solution.py:219
  77.7 3.5 all-to-all-done.1
  82.4 244.8 %attend_last.2 = bf16[256,512]{1,0:T(8,128)(2,1)S(1)} custom-call(s32[2]{0:T(128)S(1)} %pad_add_fusion.at_ref, f32[8]{0:T(128)S(1)} %dynamic_slice.33.sink_ref, bf16[256,512]{1,0:T(8,128)(2,1)S(1)} %bitcast.110, bf16[384,128]{1,0:T(8,128)(2,1)S(1)} %bitcast.112, bf16[8192,128]{1,0:T(8,128)(2,1)S(1)} %bitcast.102, bf16[8192,128]{1,0:T(8,128)(2,1)} %bitcast.12.kv_far_ref, ...), custom_call_target="tpu_custom_call" | custom-call | flops 17179869184 | bytes 2097152 | tf_op jit(solution)/shard_map/attend_last/pallas_call | solution.py:234
  328.7 5.3 convolution_convert_fusion
  337.2 120.3 %attend_last.3 = bf16[128,512]{1,0:T(8,128)(2,1)S(1)} custom-call(s32[2]{0:T(128)S(1)} %pad_add_fusion.at_ref, f32[8]{0:T(128)S(1)} %dynamic_slice.33.sink_ref, bf16[128,512]{1,0:T(8,128)(2,1)S(1)} %fusion.7.q_ref, bf16[384,128]{1,0:T(8,128)(2,1)S(1)} %bitcast.113, bf16[8192,128]{1,0:T(8,128)(2,1)S(1)} %bitcast.103, bf16[8192,128]{1,0:T(8,128)(2,1)} %bitcast.12.kv_far_ref, ...), custom_call_target="tpu_custom_call" | custom-call | flops 8589934592 | bytes 2097152 | tf_op jit(solution)/shard_map/attend_last/pallas_call | solution.py:234
  459.9 3.6 collective-permute-start.4
  464.5 4.6 convolution_convert_fusion.1
  477.1 5.2 collective-permute-done.9
  485.8 5.7 all-to-all-start.2
  492.3 11.8 %copy.70 = bf16[1,2880,2,720]{3,1,2,0:T(8,128)(2,1)} copy(bf16[1,2880,2,720]{1,3,2,0:T(8,128)(2,1)} %collective-permute-done.10) | data formatting | bytes 16588800 | tf_op jit(solution)/shard_map/optimization_barrier | solution.py:39
  504.0 4.9 select_bitcast_fusion.down_ref
  510.4 7.5 %bitcast_select_fusion.gate_up_ref = bf16[2,2880,720]{2,1,0:T(8,128)(2,1)} fusion(bf16[2,2880,720]{2,1,0:T(8,128)(2,1)} %bitcast.114, bf16[1,2880,2,720]{3,1,2,0:T(8,128)(2,1)S(1)} %copy-done.8, pred[]{:T(512)S(6)} %ne.75), kind=kLoop, calls=%fused_computation | loop fusion | flops 4147200 | bytes 24883200 | tf_op jit(solution)/shard_map/jit(_where)/select_n | solution.py:517
  517.9 4.6 all-to-all-done.2
  525.4 4.4 collective-permute-done.12.other_ref
  531.9 14.8 %expert_rows.1 = (bf16[384,2944]{1,0:T(8,128)(2,1)S(1)}, bf16[384,2944]{1,0:T(8,128)(2,1)S(1)}) custom-call(bf16[384,2944]{1,0:T(8,128)(2,1)S(1)} %reshape.175.own_ref, bf16[384,2944]{1,0:T(8,128)(2,1)S(1)} %collective-permute-done.12.other_ref, bf16[2,2880,720]{2,1,0:T(8,128)(2,1)} %bitcast_select_fusion.gate_up_ref, bf16[720,2880]{1,0:T(8,128)(2,1)S(1)} %copy-done.1), custom_call_target="tpu_custom_call" | custom-call | flops 9555148800 | bytes 21485568 | tf_op jit(solution)/shard_map/expert_rows/pallas_call | solution.py:332
  546.9 4.3 collective-permute-done.13
  554.0 38.1 %all_to_all.20 = bf16[192,2,2944]{2,1,0:T(2,128)(2,1)} all-to-all(bf16[192,2,2944]{2,1,0:T(2,128)(2,1)} %reshape.176), channel_id=1, replica_groups=mesh['chip'=16,'core'=2,'z'=4] {'chip','z'}, dimensions={0} | all-to-all | bytes 4521984 | tf_op jit(solution)/shard_map/all_to_all | solution.py:47
  (105 shorter events, 47.5 us)
Async XLA Ops:
  0.0 491.5 %copy-start = (bf16[2880,64]{0,1:T(8,128)(2,1)S(1)}, bf16[2880,64]{0,1:T(8,128)(2,1)}, u32[]{:S(2)}) copy-start(bf16[2880,64]{0,1:T(8,128)(2,1)} %param.20) | copy-start | bytes 1105924
  2.2 14.4 %copy-start.11 = (bf16[3,64,2,128]{3,2,1,0:T(2,128)(2,1)S(1)}, bf16[3,64,2,128]{3,2,1,0:T(2,128)(2,1)}, u32[]{:S(2)}) copy-start(bf16[3,64,2,128]{3,2,1,0:T(2,128)(2,1)} %param.15) | copy-start | bytes 294916
  7.2 40.1 %collective-permute-start.1 = (bf16[16,512,128]{2,1,0:T(8,128)(2,1)}, bf16[16,512,128]{2,1,0:T(8,128)(2,1)}, u32[]{:S(2)}, u32[]{:S(2)}) collective-permute-start(bf16[16,512,128]{2,1,0:T(8,128)(2,1)} %bitcast.11), channel_id=1, source_target_pairs={{0,4},{4,0},{1,5},{5,1},{2,6},{6,2},{3,7},{7,3},{8,12},{12,8},{9,1... | collective-permute-start | bytes 6291464 | tf_op jit(solution)/shard_map/ppermute | solution.py:22
  8.5 38.8 %all-to-all-start = ((bf16[16,512,128]{2,1,0:T(8,128)(2,1)}), bf16[16,512,128]{2,1,0:T(8,128)(2,1)S(1)}, u32[]{:S(2)}, u32[]{:S(2)}) async-start(bf16[16,512,128]{2,1,0:T(8,128)(2,1)} %bitcast.104), calls=%async_computation | async-start | bytes 4194304 | tf_op jit(solution)/shard_map/all_to_all | solution.py:47
  16.8 21.7 %collective-permute-start = (bf16[3,64,640]{2,1,0:T(8,128)(2,1)S(1)}, bf16[3,64,640]{2,1,0:T(8,128)(2,1)S(1)}, u32[]{:S(2)}, u32[]{:S(2)}) collective-permute-start(bf16[3,64,640]{2,1,0:T(8,128)(2,1)S(1)} %select_bitcast_fusion.1), channel_id=1, source_target_pairs={{0,4},{4,0},{1,5},{5,1},{2,6},{6,2},{3,7},{7,3},{8,12},{12,8},{9,1... | collective-permute-start | bytes 737288 | tf_op jit(solution)/shard_map/ppermute | solution.py:22
  16.9 466.6 %collective-permute-start.11 = (bf16[1,720,2880]{2,1,0:T(8,128)(2,1)}, bf16[1,720,2880]{2,1,0:T(8,128)(2,1)}, u32[]{:S(2)}, u32[]{:S(2)}) collective-permute-start(bf16[1,720,2880]{2,1,0:T(8,128)(2,1)} %param.23), channel_id=1, source_target_pairs={{4,1},{1,4},{6,3},{3,6},{12,9},{9,12},{14,11},{11,14},{20,17},{17,... | collective-permute-start | bytes 12441608 | tf_op jit(solution)/shard_map/ppermute | solution.py:35
  19.6 463.8 %collective-permute-start.10 = (bf16[1,2880,2,720]{1,3,2,0:T(8,128)(2,1)}, bf16[1,2880,2,720]{1,3,2,0:T(8,128)(2,1)}, u32[]{:S(2)}, u32[]{:S(2)}) collective-permute-start(bf16[1,2880,2,720]{1,3,2,0:T(8,128)(2,1)} %param.22), channel_id=1, source_target_pairs={{4,1},{1,4},{6,3},{3,6},{12,9},{9,12},{14,11},{11,14},{20,17},{17,... | collective-permute-start | bytes 24883208 | tf_op jit(solution)/shard_map/ppermute | solution.py:35
  23.7 12.1 %copy-start.12 = (bf16[2880]{0:T(1024)(128)(2,1)S(1)}, bf16[2880]{0:T(1024)(128)(2,1)}, u32[]{:S(2)}) copy-start(bf16[2880]{0:T(1024)(128)(2,1)} %param.18) | copy-start | bytes 17284
  23.8 12.7 %copy-start.14 = (f32[64]{0:T(128)S(1)}, f32[64]{0:T(128)}, u32[]{:S(2)}) copy-start(f32[64]{0:T(128)} %param.16) | copy-start | bytes 772
  47.3 33.8 %all-to-all-start.1 = ((bf16[16,512,128]{2,1,0:T(8,128)(2,1)}), bf16[16,512,128]{2,1,0:T(8,128)(2,1)}, u32[]{:S(2)}, u32[]{:S(2)}) async-start(bf16[16,512,128]{2,1,0:T(8,128)(2,1)} %collective-permute-done.1), calls=%async_computation.1 | async-start | bytes 4194304 | tf_op jit(solution)/shard_map/all_to_all | solution.py:47
  327.2 1.4 collective-permute-start.2
  337.2 120.6 %copy-start.9 = (bf16[128,2880]{1,0:T(8,128)(2,1)S(1)}, bf16[128,2880]{1,0:T(8,128)(2,1)}, u32[]{:S(2)}) copy-start(bf16[128,2880]{1,0:T(8,128)(2,1)} %copy.66) | copy-start | bytes 2211844
  457.6 19.2 %slice-start = ((bf16[3,16,2880]{2,1,0:T(8,128)(2,1)}), bf16[2,16,2880]{2,1,0:T(8,128)(2,1)S(1)}, s32[]{:S(2)}) async-start(bf16[3,16,2880]{2,1,0:T(8,128)(2,1)} %param.17), calls=%async_computation.4 | async-start | bytes 376832 | tf_op jit(solution)/shard_map/slice | solution.py:446
  457.6 5.9 collective-permute-start.6
  457.9 11.2 %collective-permute-start.5 = (bf16[32,2880]{1,0:T(8,128)(2,1)S(1)}, bf16[32,2880]{1,0:T(8,128)(2,1)S(1)}, u32[]{:S(2)}, u32[]{:S(2)}) collective-permute-start(bf16[32,2880]{1,0:T(8,128)(2,1)S(1)} %get-tuple-element.55), channel_id=1, source_target_pairs={{0,1},{1,2},{2,3},{3,0},{4,5},{5,6},{6,7},{7,4},{8,9},{9,10},{10,1... | collective-permute-start | bytes 552968 | tf_op jit(solution)/shard_map/ppermute | solution.py:27
  459.9 12.6 %collective-permute-start.4 = (bf16[32,2880]{1,0:T(8,128)(2,1)S(1)}, bf16[32,2880]{1,0:T(8,128)(2,1)S(1)}, u32[]{:S(2)}, u32[]{:S(2)}) collective-permute-start(bf16[32,2880]{1,0:T(8,128)(2,1)S(1)} %get-tuple-element.56), channel_id=1, source_target_pairs={{0,2},{1,3},{2,0},{3,1},{4,6},{5,7},{6,4},{7,5},{8,10},{9,11},{10,... | collective-permute-start | bytes 552968 | tf_op jit(solution)/shard_map/ppermute | solution.py:27
  463.5 18.8 %copy-start.10 = (bf16[3,16,2880]{2,1,0:T(8,128)(2,1)S(1)}, bf16[3,16,2880]{2,1,0:T(8,128)(2,1)}, u32[]{:S(2)}) copy-start(bf16[3,16,2880]{2,1,0:T(8,128)(2,1)} %param.17) | copy-start | bytes 829444
  463.5 9.0 %collective-permute-start.3 = (bf16[32,2880]{1,0:T(8,128)(2,1)S(1)}, bf16[32,2880]{1,0:T(8,128)(2,1)S(1)}, u32[]{:S(2)}, u32[]{:S(2)}) collective-permute-start(bf16[32,2880]{1,0:T(8,128)(2,1)S(1)} %get-tuple-element.57), channel_id=1, source_target_pairs={{0,3},{1,0},{2,1},{3,2},{4,7},{5,4},{6,5},{7,6},{8,11},{9,8},{10,9... | collective-permute-start | bytes 552968 | tf_op jit(solution)/shard_map/ppermute | solution.py:27
  472.5 4.6 collective-permute-start.7
  474.7 7.6 %collective-permute-start.9 = (bf16[16,2880]{1,0:T(8,128)(2,1)S(1)}, bf16[16,2880]{1,0:T(8,128)(2,1)S(1)}, u32[]{:S(2)}, u32[]{:S(2)}) collective-permute-start(bf16[16,2880]{1,0:T(8,128)(2,1)S(1)} %get-tuple-element.64), channel_id=1, source_target_pairs={{0,1},{1,2},{2,3},{3,0},{4,5},{5,6},{6,7},{7,4},{8,9},{9,10},{10,1... | collective-permute-start | bytes 276488 | tf_op jit(solution)/shard_map/ppermute | solution.py:27
  474.7 7.6 %collective-permute-start.8 = (bf16[16,2880]{1,0:T(8,128)(2,1)S(1)}, bf16[16,2880]{1,0:T(8,128)(2,1)S(1)}, u32[]{:S(2)}, u32[]{:S(2)}) collective-permute-start(bf16[16,2880]{1,0:T(8,128)(2,1)S(1)} %get-tuple-element.65), channel_id=1, source_target_pairs={{0,2},{1,3},{2,0},{3,1},{4,6},{5,7},{6,4},{7,5},{8,10},{9,11},{10,... | collective-permute-start | bytes 276488 | tf_op jit(solution)/shard_map/ppermute | solution.py:27
  485.8 36.7 %all-to-all-start.2 = ((bf16[192,2,2944]{2,1,0:T(2,128)(2,1)}), bf16[192,2,2944]{2,1,0:T(2,128)(2,1)}, u32[]{:S(2)}, u32[]{:S(2)}) async-start(bf16[192,2,2944]{2,1,0:T(2,128)(2,1)} %reshape.174), calls=%async_computation.2 | async-start | bytes 4521984 | tf_op jit(solution)/shard_map/all_to_all | solution.py:47
  525.3 4.5 collective-permute-start.12
  546.7 4.5 collective-permute-start.13
  (9 other events, 28.2 us)
